TPU v7x, 32 devices: a whole 2x2x4 slice. The times are simulated.
32 devices in a mesh: section: 2 (over x), fsdp: 16 (over z, y, core).
Axes of the slice: x: 2, y: 2, z: 4, core: 2. Of those that a mesh axis runs over, the one named last changes fastest.
Arguments:
- block_input: bfloat16 [2, 4096, 1024], P(None, 'fsdp'), may hold values from -6 to 6
- output_grad: bfloat16 [2, 4096, 1024], P(None, 'fsdp'), may hold values from -6 to 6
- document_ids: int32 [2, 4096], P(None, 'fsdp'), may hold values from 0 to 63, never falling along the last dimension, each value on 1 to 128 neighbouring positions
- memory_keys: bfloat16 [2, 16384, 1024], P(None, 'fsdp'), may hold values from -6 to 6
- memory_values: bfloat16 [2, 16384, 1024], P(None, 'fsdp'), may hold values from -6 to 6
- memory_index: int32 [2, 64, 128], P(None, 'fsdp'), may hold values from 0 to 1023
- memory_reset: int32 [2, 64], P(None, 'fsdp'), may hold values 0 or 1
- query_weight: bfloat16 [2, 1024, 1024], P('section', 'fsdp'), may hold values from -0.1875 to 0.1875
- key_weight: bfloat16 [2, 1024, 1024], P('section', 'fsdp'), may hold values from -0.1875 to 0.1875
- value_weight: bfloat16 [2, 1024, 1024], P('section', 'fsdp'), may hold values from -0.1875 to 0.1875
- output_weight: bfloat16 [2, 1024, 1024], P('section', 'fsdp'), may hold values from -1 to 1
- gate_weight: bfloat16 [2, 1024, 2816], P('section', 'fsdp'), may hold values from -0.1875 to 0.1875
- up_weight: bfloat16 [2, 1024, 2816], P('section', 'fsdp'), may hold values from -0.1875 to 0.1875
- down_weight: bfloat16 [2, 2816, 1024], P('section', 'fsdp'), may hold values from -0.109375 to 0.109375
- attend_gain: bfloat16 [2, 1024], P('section', 'fsdp'), may hold values from 0.099609375 to 1.8984375
- feed_gain: bfloat16 [2, 1024], P('section', 'fsdp'), may hold values from 0.099609375 to 1.8984375
Outputs:
- section_output: bfloat16 [2, 2, 4096, 1024], P('section', None, 'fsdp')
- input_grad: bfloat16 [2, 2, 4096, 1024], P('section', None, 'fsdp')
- grad_query: bfloat16 [2, 1024, 1024], P('section', 'fsdp')
- grad_key: bfloat16 [2, 1024, 1024], P('section', 'fsdp')
- grad_value: bfloat16 [2, 1024, 1024], P('section', 'fsdp')
- grad_output: bfloat16 [2, 1024, 1024], P('section', 'fsdp')
- grad_gate: bfloat16 [2, 1024, 2816], P('section', 'fsdp')
- grad_up: bfloat16 [2, 1024, 2816], P('section', 'fsdp')
- grad_down: bfloat16 [2, 2816, 1024], P('section', 'fsdp')
- grad_attend: bfloat16 [2, 1024], P('section', 'fsdp')
- grad_feed: bfloat16 [2, 1024], P('section', 'fsdp')
Inputs may be any that keep to these rules, and one draw needn't show every extreme that they name: `memory_index`: indices into the sequence's own 1024 cache rows. `document_ids`: never falling along a micro-batch's tokens.
All inputs are finite; a program needn't handle non-finite values. No bound on the sum of `memory_reset` on one device may be relied on, other than what follows from the above.
Results may differ from a plain program's by a relative error of at most 0.02.
Values may be sent and summed in bfloat16 or wider, within the bound.
A program may use at most 256 MiB of HBM per device.

v0:
```python
import jax
import jax.numpy as jnp
from jax import lax
from jax.sharding import PartitionSpec as P

HEADS = 8
HD = 128
MQB = 64
MEMK = 128


EPS = 1e-06
MASKED = -1e30


def passed_along(array, axis, by):
    length = lax.axis_size(axis)
    pairs = [(i, i + by) for i in range(length) if 0 <= i + by < length]
    return lax.ppermute(array, axis, pairs)


def forward_product(left, right):
    return jnp.dot(left, right, preferred_element_type=jnp.float32)


def outer_sum(left, right):
    return lax.dot_general(
        left, right, (((0,), (0,)), ((), ())), preferred_element_type=jnp.float32
    )


def back_product(left, right):
    return lax.dot_general(
        left, right, (((1,), (1,)), ((), ())), preferred_element_type=jnp.float32
    )


def norm_scale(rows):
    return lax.rsqrt(jnp.mean(rows * rows, axis=-1, keepdims=True) + EPS)


def norm_back(rows, inverse, gain, upstream):
    scaled = upstream * gain
    rows_grad = inverse * scaled - rows * inverse**3 * jnp.mean(
        scaled * rows, axis=-1, keepdims=True
    )
    gain_grad = jnp.sum(upstream * rows * inverse, axis=0)
    return (rows_grad, gain_grad)


def store(buffer, value, pick, valid):
    previous = lax.dynamic_index_in_dim(buffer, pick, 0, keepdims=False)
    return lax.dynamic_update_index_in_dim(buffer, jnp.where(valid, value, previous), pick, 0)


def recall(cache_keys, cache_values, memory_index, pick):
    flat = lax.dynamic_index_in_dim(memory_index, pick, 0, keepdims=False).reshape(-1)
    keys_here = lax.dynamic_index_in_dim(cache_keys, pick, 0, keepdims=False)
    values_here = lax.dynamic_index_in_dim(cache_values, pick, 0, keepdims=False)
    return (jnp.take(keys_here, flat, axis=0), jnp.take(values_here, flat, axis=0))


def layer_forward(weights, inputs, documents, remote_keys, remote_values, live):
    (
        query_weight,
        key_weight,
        value_weight,
        output_weight,
        gate_weight,
        up_weight,
        down_weight,
        attend_gain,
        feed_gain,
    ) = weights
    rows = inputs.shape[0]
    blocks = rows // MQB
    scale = HD ** (-0.5)
    first_inv = norm_scale(inputs)
    normed = (inputs * first_inv * attend_gain.astype(jnp.float32)).astype(jnp.bfloat16)
    queries = forward_product(normed, query_weight).astype(jnp.bfloat16).reshape(rows, HEADS, HD)
    keys = forward_product(normed, key_weight).astype(jnp.bfloat16).reshape(rows, HEADS, HD)
    values = forward_product(normed, value_weight).astype(jnp.bfloat16).reshape(rows, HEADS, HD)
    local = jnp.einsum("qhd,khd->hqk", queries, keys, preferred_element_type=jnp.float32) * scale
    position = jnp.arange(rows)
    allowed = (position[None, :] <= position[:, None]) & (documents[None, :] == documents[:, None])
    local = jnp.where(allowed[None], local, MASKED)
    key_blocks = remote_keys.reshape(blocks, MEMK, HEADS, HD)
    value_blocks = remote_values.reshape(blocks, MEMK, HEADS, HD)
    recalled = (
        jnp.einsum(
            "bqhd,bkhd->hbqk",
            queries.reshape(blocks, MQB, HEADS, HD),
            key_blocks,
            preferred_element_type=jnp.float32,
        )
        * scale
    )
    recalled = jnp.where(live[None, :, None, None], recalled, MASKED)
    top = jnp.maximum(jnp.max(local, axis=-1), jnp.max(recalled, axis=-1).reshape(HEADS, rows))
    local_exp = jnp.exp(local - top[:, :, None])
    recalled_exp = jnp.exp(recalled - top.reshape(HEADS, blocks, MQB)[..., None])
    total = jnp.sum(local_exp, axis=-1) + jnp.sum(recalled_exp, axis=-1).reshape(HEADS, rows)
    local_prob = local_exp / total[:, :, None]
    recalled_prob = recalled_exp / total.reshape(HEADS, blocks, MQB)[..., None]
    mixed = jnp.einsum(
        "hqk,khd->qhd", local_prob.astype(jnp.bfloat16), values, preferred_element_type=jnp.float32
    )
    mixed = mixed + jnp.einsum(
        "hbqk,bkhd->bqhd",
        recalled_prob.astype(jnp.bfloat16),
        value_blocks,
        preferred_element_type=jnp.float32,
    ).reshape(rows, HEADS, HD)
    mixed = mixed.reshape(rows, HEADS * HD).astype(jnp.bfloat16)
    middle = inputs + forward_product(mixed, output_weight)
    second_inv = norm_scale(middle)
    normed_two = (middle * second_inv * feed_gain.astype(jnp.float32)).astype(jnp.bfloat16)
    gate = forward_product(normed_two, gate_weight)
    up = forward_product(normed_two, up_weight)
    hidden = (jax.nn.silu(gate) * up).astype(jnp.bfloat16)
    result = middle + forward_product(hidden, down_weight)
    saved = (
        first_inv,
        normed,
        queries,
        keys,
        values,
        key_blocks,
        value_blocks,
        local_prob,
        recalled_prob,
        mixed,
        middle,
        second_inv,
        normed_two,
        gate,
        up,
        hidden,
    )
    return (result, saved)


def layer_backward(weights, inputs, saved, upstream):
    (
        query_weight,
        key_weight,
        value_weight,
        output_weight,
        gate_weight,
        up_weight,
        down_weight,
        attend_gain,
        feed_gain,
    ) = weights
    (
        first_inv,
        normed,
        queries,
        keys,
        values,
        key_blocks,
        value_blocks,
        local_prob,
        recalled_prob,
        mixed,
        middle,
        second_inv,
        normed_two,
        gate,
        up,
        hidden,
    ) = saved
    rows = inputs.shape[0]
    blocks = rows // MQB
    scale = HD ** (-0.5)
    down_in = upstream.astype(jnp.bfloat16)
    down_sum = outer_sum(hidden, down_in)
    hidden_grad = back_product(down_in, down_weight)
    sigma = jax.nn.sigmoid(gate)
    up_in = (hidden_grad * gate * sigma).astype(jnp.bfloat16)
    gate_in = (hidden_grad * up * sigma * (1.0 + gate * (1.0 - sigma))).astype(jnp.bfloat16)
    gate_sum = outer_sum(normed_two, gate_in)
    up_sum = outer_sum(normed_two, up_in)
    normed_two_grad = back_product(gate_in, gate_weight) + back_product(up_in, up_weight)
    middle_part, feed_sum = norm_back(
        middle, second_inv, feed_gain.astype(jnp.float32), normed_two_grad
    )
    middle_grad = upstream + middle_part
    attend_in = middle_grad.astype(jnp.bfloat16)
    output_sum = outer_sum(mixed, attend_in)
    mixed_grad = (
        back_product(attend_in, output_weight).astype(jnp.bfloat16).reshape(rows, HEADS, HD)
    )
    mixed_blocks = mixed_grad.reshape(blocks, MQB, HEADS, HD)
    values_grad = jnp.einsum(
        "hqk,qhd->khd",
        local_prob.astype(jnp.bfloat16),
        mixed_grad,
        preferred_element_type=jnp.float32,
    )
    local_pgrad = jnp.einsum("qhd,khd->hqk", mixed_grad, values, preferred_element_type=jnp.float32)
    recalled_pgrad = jnp.einsum(
        "bqhd,bkhd->hbqk", mixed_blocks, value_blocks, preferred_element_type=jnp.float32
    )
    weighted = jnp.sum(local_prob * local_pgrad, axis=-1) + jnp.sum(
        recalled_prob * recalled_pgrad, axis=-1
    ).reshape(HEADS, rows)
    local_sgrad = (local_prob * (local_pgrad - weighted[:, :, None])).astype(jnp.bfloat16)
    recalled_sgrad = (
        recalled_prob * (recalled_pgrad - weighted.reshape(HEADS, blocks, MQB)[..., None])
    ).astype(jnp.bfloat16)
    queries_total = jnp.einsum(
        "hqk,khd->qhd", local_sgrad, keys, preferred_element_type=jnp.float32
    )
    queries_total = queries_total + jnp.einsum(
        "hbqk,bkhd->bqhd", recalled_sgrad, key_blocks, preferred_element_type=jnp.float32
    ).reshape(rows, HEADS, HD)
    queries_grad = (queries_total * scale).astype(jnp.bfloat16).reshape(rows, HEADS * HD)
    keys_grad = (
        (
            jnp.einsum("hqk,qhd->khd", local_sgrad, queries, preferred_element_type=jnp.float32)
            * scale
        )
        .astype(jnp.bfloat16)
        .reshape(rows, HEADS * HD)
    )
    values_grad = values_grad.astype(jnp.bfloat16).reshape(rows, HEADS * HD)
    query_sum = outer_sum(normed, queries_grad)
    key_sum = outer_sum(normed, keys_grad)
    value_sum = outer_sum(normed, values_grad)
    normed_grad = (
        back_product(queries_grad, query_weight)
        + back_product(keys_grad, key_weight)
        + back_product(values_grad, value_weight)
    )
    input_part, attend_sum = norm_back(
        inputs, first_inv, attend_gain.astype(jnp.float32), normed_grad
    )
    layer_grad = middle_grad + input_part
    return (
        layer_grad,
        (
            query_sum,
            key_sum,
            value_sum,
            output_sum,
            gate_sum,
            up_sum,
            down_sum,
            attend_sum,
            feed_sum,
        ),
    )


def per_device(
    block_input,
    output_grad,
    document_ids,
    memory_keys,
    memory_values,
    memory_index,
    memory_reset,
    query_weight,
    key_weight,
    value_weight,
    output_weight,
    gate_weight,
    up_weight,
    down_weight,
    attend_gain,
    feed_gain,
):
    section = lax.axis_index("section")
    micro = block_input.shape[0]
    ticks = micro + lax.axis_size("section") - 1
    weights = (
        lax.all_gather(query_weight[0], "fsdp", axis=0, tiled=True),
        lax.all_gather(key_weight[0], "fsdp", axis=0, tiled=True),
        lax.all_gather(value_weight[0], "fsdp", axis=0, tiled=True),
        lax.all_gather(output_weight[0], "fsdp", axis=0, tiled=True),
        lax.all_gather(gate_weight[0], "fsdp", axis=0, tiled=True),
        lax.all_gather(up_weight[0], "fsdp", axis=0, tiled=True),
        lax.all_gather(down_weight[0], "fsdp", axis=0, tiled=True),
        lax.all_gather(attend_gain[0], "fsdp", axis=0, tiled=True),
        lax.all_gather(feed_gain[0], "fsdp", axis=0, tiled=True),
    )
    kept_in = jnp.zeros_like(block_input)
    kept_out = jnp.zeros_like(block_input)
    arrived = jnp.zeros(block_input.shape[1:], jnp.bfloat16)
    for tick in range(ticks):
        order = tick - section
        valid = (order >= 0) & (order < micro)
        pick = jnp.clip(order, 0, micro - 1)
        own = lax.dynamic_index_in_dim(block_input, pick, 0, keepdims=False)
        current = jnp.where(section == 0, own, arrived)
        documents = lax.dynamic_index_in_dim(document_ids, pick, 0, keepdims=False)
        live = (section == 1) & (
            lax.dynamic_index_in_dim(memory_reset, pick, 0, keepdims=False) == 0
        )
        remote_keys, remote_values = recall(memory_keys, memory_values, memory_index, pick)
        result, saved = layer_forward(
            weights, current.astype(jnp.float32), documents, remote_keys, remote_values, live
        )
        sent = result.astype(jnp.bfloat16)
        kept_in = store(kept_in, current, pick, valid)
        kept_out = store(kept_out, sent, pick, valid)
        if tick + 1 < ticks:
            arrived = passed_along(sent, "section", 1)
    shard_list = (
        query_weight[0],
        key_weight[0],
        value_weight[0],
        output_weight[0],
        gate_weight[0],
        up_weight[0],
        down_weight[0],
        attend_gain[0],
        feed_gain[0],
    )
    totals = tuple((jnp.zeros(w.shape, jnp.float32) for w in weights))
    shares = tuple((jnp.zeros(s.shape, jnp.float32) for s in shard_list))
    grads_in = jnp.zeros_like(block_input)
    returned = jnp.zeros(block_input.shape[1:], jnp.bfloat16)
    for tick in range(ticks):
        order = tick - (1 - section)
        valid = (order >= 0) & (order < micro)
        pick = jnp.clip(order, 0, micro - 1)
        own = lax.dynamic_index_in_dim(output_grad, pick, 0, keepdims=False)
        upstream = jnp.where(section == 1, own, returned).astype(jnp.float32)
        upstream = jnp.where(valid, upstream, 0.0)
        current = lax.dynamic_index_in_dim(kept_in, pick, 0, keepdims=False).astype(jnp.float32)
        documents = lax.dynamic_index_in_dim(document_ids, pick, 0, keepdims=False)
        live = (section == 1) & (
            lax.dynamic_index_in_dim(memory_reset, pick, 0, keepdims=False) == 0
        )
        remote_keys, remote_values = recall(memory_keys, memory_values, memory_index, pick)
        result, saved = layer_forward(weights, current, documents, remote_keys, remote_values, live)
        layer_grad, sums = layer_backward(weights, current, saved, upstream)
        sent_back = layer_grad.astype(jnp.bfloat16)
        grads_in = store(grads_in, sent_back, pick, valid)
        totals = tuple((a + b for a, b in zip(totals, sums)))
        if tick + 1 < ticks:
            returned = passed_along(sent_back, "section", -1)
    (
        query_total,
        key_total,
        value_total,
        output_total,
        gate_total,
        up_total,
        down_total,
        attend_total,
        feed_total,
    ) = totals
    shares = (
        lax.psum_scatter(query_total, "fsdp", scatter_dimension=0, tiled=True),
        lax.psum_scatter(key_total, "fsdp", scatter_dimension=0, tiled=True),
        lax.psum_scatter(value_total, "fsdp", scatter_dimension=0, tiled=True),
        lax.psum_scatter(output_total, "fsdp", scatter_dimension=0, tiled=True),
        lax.psum_scatter(gate_total, "fsdp", scatter_dimension=0, tiled=True),
        lax.psum_scatter(up_total, "fsdp", scatter_dimension=0, tiled=True),
        lax.psum_scatter(down_total, "fsdp", scatter_dimension=0, tiled=True),
        lax.psum_scatter(attend_total, "fsdp", scatter_dimension=0, tiled=True),
        lax.psum_scatter(feed_total, "fsdp", scatter_dimension=0, tiled=True),
    )
    results = tuple((s.astype(jnp.bfloat16)[None] for s in shares))
    return (
        kept_out[None],
        grads_in[None],
        results[0],
        results[1],
        results[2],
        results[3],
        results[4],
        results[5],
        results[6],
        results[7],
        results[8],
    )


def solution(mesh):
    placed = (
        P(None, "fsdp", None),
        P(None, "fsdp", None),
        P(None, "fsdp"),
        P(None, "fsdp", None),
        P(None, "fsdp", None),
        P(None, "fsdp", None),
        P(None, "fsdp"),
        P("section", "fsdp", None),
        P("section", "fsdp", None),
        P("section", "fsdp", None),
        P("section", "fsdp", None),
        P("section", "fsdp", None),
        P("section", "fsdp", None),
        P("section", "fsdp", None),
        P("section", "fsdp"),
        P("section", "fsdp"),
    )
    return jax.shard_map(
        per_device,
        mesh=mesh,
        in_specs=placed,
        out_specs=(
            P("section", None, "fsdp", None),
            P("section", None, "fsdp", None),
            P("section", "fsdp", None),
            P("section", "fsdp", None),
            P("section", "fsdp", None),
            P("section", "fsdp", None),
            P("section", "fsdp", None),
            P("section", "fsdp", None),
            P("section", "fsdp", None),
            P("section", "fsdp"),
            P("section", "fsdp"),
        ),
        check_vma=False,
    )
```

profile of v0, /device:TPU:0, one launch (start us, length us, event | category | flops | bytes accessed | tf_op | source)
XLA Modules:
  0.0 1390.3 jit_solution(1059721422290177813)
XLA Ops:
  13.3 16.6 %dynamic-slice_bitcast_fusion = (bf16[1024,1024]{1,0:T(8,128)(2,1)S(1)}, bf16[1024,1024]{1,0:T(8,128)(2,1)}, bf16[1024,1024]{1,0:T(8,128)(2,1)}, bf16[1024,1024]...) fusion(bf16[2,1024,1024]{2,1,0:T(8,128)(2,1)} %param.22, ...), kind=kLoop, calls=%fused_computation.159 | loop fusion | bytes 50331672 | tf_op jit(solution)/shard_map/jit(dynamic_index_in_dim)/squeeze | solution.py:59
  30.0 4.6 gather_fusion
  34.6 5.3 gather_fusion.1
  45.6 35.3 %all-reduce.5 = (bf16[1024]{0:T(1024)(128)(2,1)S(1)}, bf16[1024]{0:T(1024)(128)(2,1)S(1)}) all-reduce(bf16[1024]{0:T(1024)(128)(2,1)S(1)} %dynamic-update-slice, bf16[1024]{0:T(1024)(128)(2,1)S(1)} %dynamic-update-slice.1), channel_id=2, replica_groups=mesh['section'=2,'fsdp'=16] {'fsdp'}, use_global_device_ids=true, to_apply=%add | all-reduce | flops 2048 | bytes 8192
  80.9 5.3 gather_fusion.2
  86.2 5.4 gather_fusion.3
  92.2 5.4 gather_fusion.6
  97.6 5.3 gather_fusion.7
  102.9 5.3 gather_fusion.8
  108.2 5.4 gather_fusion.9
  113.6 5.3 gather_fusion.10
  157.2 24.1 %all-gather.23.cloned.1.call-done = bf16[1,1024,1024]{2,1,0:T(8,128)(2,1)} async-done(((bf16[1,64,1024]{2,1,0:T(8,128)(2,1)}), bf16[1,1024,1024]{2,1,0:T(8,128)(2,1)}) %all-gather.23.cloned.1.call-update) | async-done | bytes 2097168 | tf_op jit(solution)/shard_map/all_gather | solution.py:281
  183.9 57.4 %all-gather.25.cloned.1.call-done = bf16[1,1024,2816]{2,1,0:T(8,128)(2,1)} async-done(((bf16[1,64,2816]{2,1,0:T(8,128)(2,1)}), bf16[1,1024,2816]{2,1,0:T(8,128)(2,1)}) %all-gather.25.cloned.1.call-update) | async-done | bytes 5767184 | tf_op jit(solution)/shard_map/all_gather | solution.py:282
  241.2 5.9 fusion.46
  247.1 53.9 %all-gather.29.cloned.1.call-done = bf16[1,2816,1024]{2,1,0:T(8,128)(2,1)} async-done(((bf16[1,176,1024]{2,1,0:T(8,128)(2,1)}), bf16[1,2816,1024]{2,1,0:T(8,128)(2,1)}) %all-gather.29.cloned.1.call-update) | async-done | bytes 5767184 | tf_op jit(solution)/shard_map/all_gather | solution.py:284
  301.0 60.0 %all-gather.27.cloned.1.call-done = bf16[1,1024,2816]{2,1,0:T(8,128)(2,1)} async-done(((bf16[1,64,2816]{2,1,0:T(8,128)(2,1)}), bf16[1,1024,2816]{2,1,0:T(8,128)(2,1)}) %all-gather.27.cloned.1.call-update) | async-done | bytes 5767184 | tf_op jit(solution)/shard_map/all_gather | solution.py:283
  361.1 9.5 bitcast_dynamic-update-slice_fusion.5
  371.6 4.3 collective-permute-start
  412.5 5.9 fusion.44
  418.5 10.3 bitcast_dynamic-update-slice_fusion.4
  430.6 6.1 fusion.4
  436.7 5.4 collective-permute-done.1
  478.0 4.1 multiply_convert_fusion.8
  491.3 4.0 multiply_reduce_fusion.2
  554.5 4.9 fusion.36
  567.7 5.4 fusion.16
  580.5 4.1 multiply_reduce_fusion.1
  642.4 5.1 fusion.32
  654.8 5.4 fusion.12
  667.7 4.4 multiply_reduce_fusion
  717.4 6.1 fusion.620
  723.5 10.7 add_add_fusion.2
  734.3 3.4 fusion.621
  737.8 6.0 fusion.622
  743.7 10.7 add_add_fusion.1
  754.8 9.0 fusion.153
  763.9 6.0 fusion.154
  769.8 14.4 %add_add_fusion = f32[2816,1024]{1,0:T(8,128)} fusion(f32[2816,1024]{1,0:T(8,128)} %fusion.153, f32[2816,1024]{1,0:T(8,128)} %fusion.154, f32[256,2816]{1,0:T(8,128)S(1)} %copy-done.89, f32[256,2816]{1,0:T(8,128)S(1)} %copy-done.87, bf16[256,1024]{1,0:T(8,128)(2,1)S(1)} %copy-done.44, pred[]{:T(512)S(6)} %and.154), kind=kOutput, calls=%fused_computation.12 | convolution fusion | flops 1487273984 | bytes 40894464 | tf_op jit(solution)/shard_map/dot_general | solution.py:27
  784.9 5.4 gather_fusion.4
  790.3 5.6 gather_fusion.5
  833.4 6.1 fusion.42
  839.5 9.8 fusion.350
  857.8 30.6 %all-reduce.4 = (bf16[1024]{0:T(1024)(128)(2,1)S(1)}, bf16[1024]{0:T(1024)(128)(2,1)S(1)}) all-reduce(f32[1024]{0:T(1024)S(1)} %add_add_fusion.8, f32[1024]{0:T(1024)S(1)} %add_add_fusion.7), channel_id=18, replica_groups=mesh['section'=2,'fsdp'=16] {'fsdp'}, use_global_device_ids=true, to_apply=%region_58.60.clone | all-reduce | flops 2048 | bytes 12288
  895.3 20.1 %reduce-scatter.12.cloned.1.call-done = f32[64,1024]{1,0:T(8,128)} async-done(((f32[1024,1024]{1,0:T(8,128)}), f32[64,1024]{1,0:T(8,128)}) %reduce-scatter.12.cloned.1.call-update) | async-done | bytes 262160 | tf_op jit(solution)/shard_map/reduce_scatter | solution.py:359
  917.0 74.3 %reduce-scatter.14.cloned.1.call-done = f32[64,1024]{1,0:T(8,128)} async-done(((f32[1024,1024]{1,0:T(8,128)}), f32[64,1024]{1,0:T(8,128)}) %reduce-scatter.14.cloned.1.call-update) | async-done | bytes 262160 | tf_op jit(solution)/shard_map/reduce_scatter | solution.py:360
  992.9 127.6 %reduce-scatter.16.cloned.1.call-done = f32[64,2816]{1,0:T(8,128)} async-done(((f32[1024,2816]{1,0:T(8,128)}), f32[64,2816]{1,0:T(8,128)}) %reduce-scatter.16.cloned.1.call-update) | async-done | bytes 720912 | tf_op jit(solution)/shard_map/reduce_scatter | solution.py:361
  1122.5 128.8 %reduce-scatter.18.cloned.1.call-done = f32[64,2816]{1,0:T(8,128)} async-done(((f32[1024,2816]{1,0:T(8,128)}), f32[64,2816]{1,0:T(8,128)}) %reduce-scatter.18.cloned.1.call-update) | async-done | bytes 720912 | tf_op jit(solution)/shard_map/reduce_scatter | solution.py:362
  1253.2 128.2 %reduce-scatter.20.cloned.1.call-done = f32[176,1024]{1,0:T(8,128)} async-done(((f32[2816,1024]{1,0:T(8,128)}), f32[176,1024]{1,0:T(8,128)}) %reduce-scatter.20.cloned.1.call-update) | async-done | bytes 720912 | tf_op jit(solution)/shard_map/reduce_scatter | solution.py:363
  (716 shorter events, 389.8 us)
Async XLA Ops:
  7.2 126.3 %all-gather.19.cloned.1.call-start = ((), (), s32[]{:S(2)}) async-start(), calls=%async_computation.15 | async-start | bytes 2228224 | tf_op jit(solution)/shard_map/all_gather | solution.py:278
  7.9 130.1 %all-gather.21.cloned.1.call-start = ((), (), s32[]{:S(2)}) async-start(), calls=%async_computation.16 | async-start | bytes 2228224 | tf_op jit(solution)/shard_map/all_gather | solution.py:279
  8.7 140.2 %all-gather.17.cloned.1.call-start = ((), (), s32[]{:S(2)}) async-start(), calls=%async_computation.14 | async-start | bytes 2228224 | tf_op jit(solution)/shard_map/all_gather | solution.py:280
  9.4 171.9 %all-gather.23.cloned.1.call-start = ((), (), s32[]{:S(2)}) async-start(), calls=%async_computation.17 | async-start | bytes 2228224 | tf_op jit(solution)/shard_map/all_gather | solution.py:281
  10.0 231.3 %all-gather.25.cloned.1.call-start = ((), (), s32[]{:S(2)}) async-start(), calls=%async_computation.18 | async-start | bytes 6127616 | tf_op jit(solution)/shard_map/all_gather | solution.py:282
  10.6 290.5 %all-gather.29.cloned.1.call-start = ((), (), s32[]{:S(2)}) async-start(), calls=%async_computation.20 | async-start | bytes 6127616 | tf_op jit(solution)/shard_map/all_gather | solution.py:284
  11.1 349.9 %all-gather.27.cloned.1.call-start = ((), (), s32[]{:S(2)}) async-start(), calls=%async_computation.19 | async-start | bytes 6127616 | tf_op jit(solution)/shard_map/all_gather | solution.py:283
  11.9 880.1 %reduce-scatter.8.cloned.1.call-start = ((), (), s32[]{:S(2)}) async-start(), calls=%async_computation.7 | async-start | bytes 4456448 | tf_op jit(solution)/shard_map/reduce_scatter | solution.py:357
  371.6 7.1 copy-start.76
  371.6 18.3 %collective-permute-start = (bf16[256,1024]{1,0:T(8,128)(2,1)}, bf16[256,1024]{1,0:T(8,128)(2,1)}, u32[]{:S(2)}, u32[]{:S(2)}) collective-permute-start(bf16[256,1024]{1,0:T(8,128)(2,1)} %get-tuple-element.123), channel_id=1, source_target_pairs={{0,16},{1,17},{2,18},{3,19},{4,20},{5,21},{6,22},{7,23},{8,24},{9,... | collective-permute-start | bytes 1572872 | tf_op jit(solution)/shard_map/ppermute | solution.py:19
  428.8 13.3 copy-start.34
  428.8 13.3 collective-permute-start.1
  436.7 6.8 copy-start.6
  549.8 9.6 copy-start.29
  549.9 15.2 %collective-permute-start.2 = (bf16[256,1024]{1,0:T(8,128)(2,1)S(1)}, bf16[256,1024]{1,0:T(8,128)(2,1)S(1)}, u32[]{:S(2)}, u32[]{:S(2)}) collective-permute-start(bf16[256,1024]{1,0:T(8,128)(2,1)S(1)} %get-tuple-element.37), channel_id=1, source_target_pairs={{16,0},{17,1},{18,2},{19,3},{20,4},{21,5},{22,6},{23,7},{24,8},{25... | collective-permute-start | bytes 1572872 | tf_op jit(solution)/shard_map/ppermute | solution.py:19
  553.4 6.9 slice-start.12
  554.5 10.7 slice-start.6
  560.3 12.7 slice-start.2
  565.1 10.4 copy-start.46
  565.1 7.9 slice-start.3
  611.9 6.4 copy-start.157
  638.0 14.1 %collective-permute-start.3 = (bf16[256,1024]{1,0:T(8,128)(2,1)S(1)}, bf16[256,1024]{1,0:T(8,128)(2,1)S(1)}, u32[]{:S(2)}, u32[]{:S(2)}) collective-permute-start(bf16[256,1024]{1,0:T(8,128)(2,1)S(1)} %get-tuple-element.33), channel_id=1, source_target_pairs={{16,0},{17,1},{18,2},{19,3},{20,4},{21,5},{22,6},{23,7},{24,8},{25... | collective-permute-start | bytes 1572872 | tf_op jit(solution)/shard_map/ppermute | solution.py:19
  641.4 9.0 slice-start.14
  642.4 8.0 copy-start.40
  642.4 8.0 slice-start.15
  642.4 9.8 slice-start.8
  650.4 9.8 slice-start.4
  652.3 10.5 copy-start.43
  652.3 8.0 slice-start.5
  681.4 6.6 copy-start.20
  681.4 6.6 copy-start.21
  690.9 202.7 %reduce-scatter.10.cloned.1.call-start = ((), (), s32[]{:S(2)}) async-start(), calls=%async_computation.8 | async-start | bytes 4456448 | tf_op jit(solution)/shard_map/reduce_scatter | solution.py:358
  698.6 216.7 %reduce-scatter.12.cloned.1.call-start = ((), (), s32[]{:S(2)}) async-start(), calls=%async_computation.9 | async-start | bytes 4456448 | tf_op jit(solution)/shard_map/reduce_scatter | solution.py:359
  707.0 284.3 %reduce-scatter.14.cloned.1.call-start = ((), (), s32[]{:S(2)}) async-start(), calls=%async_computation.10 | async-start | bytes 4456448 | tf_op jit(solution)/shard_map/reduce_scatter | solution.py:360
  713.9 406.7 %reduce-scatter.16.cloned.1.call-start = ((), (), s32[]{:S(2)}) async-start(), calls=%async_computation.11 | async-start | bytes 12255232 | tf_op jit(solution)/shard_map/reduce_scatter | solution.py:361
  717.4 6.1 copy-start.41
  717.4 6.1 copy-start.108
  734.2 517.1 %reduce-scatter.18.cloned.1.call-start = ((), (), s32[]{:S(2)}) async-start(), calls=%async_computation.12 | async-start | bytes 12255232 | tf_op jit(solution)/shard_map/reduce_scatter | solution.py:362
  737.7 6.0 copy-start.42
  737.8 6.0 copy-start.106
  754.5 626.8 %reduce-scatter.20.cloned.1.call-start = ((), (), s32[]{:S(2)}) async-start(), calls=%async_computation.13 | async-start | bytes 12255232 | tf_op jit(solution)/shard_map/reduce_scatter | solution.py:363
  754.8 9.1 copy-start.36
  754.8 9.1 copy-start.38
  754.8 9.1 copy-start.47
  833.4 6.1 copy-start.32
  855.8 33.8 %copy-start.19 = (f32[256,1024]{1,0:T(8,128)S(1)}, f32[256,1024]{1,0:T(8,128)}, u32[]{:S(2)}) copy-start(f32[256,1024]{1,0:T(8,128)} %copy-done.17) | copy-start | bytes 3145732
  855.8 33.8 %copy-start.30 = (bf16[2,256,1024]{2,1,0:T(8,128)(2,1)S(1)}, bf16[2,256,1024]{2,1,0:T(8,128)(2,1)}, u32[]{:S(2)}) copy-start(bf16[2,256,1024]{2,1,0:T(8,128)(2,1)} %get-tuple-element.32) | copy-start | bytes 3145732
  855.9 33.8 %copy-start.148 = (f32[256]{0:T(256)S(1)}, f32[256]{0:T(256)}, u32[]{:S(2)}) copy-start(f32[256]{0:T(256)} %get-tuple-element.84) | copy-start | bytes 3076
  (152 other events, 414.7 us)
Sparse Core Ops, SparseCore 0:
  10.2 44.0 all-gather.18
  56.5 40.1 all-gather.20
  98.8 40.1 all-gather.16
  141.1 40.1 all-gather.22
  183.4 57.7 all-gather.24
  243.4 57.6 all-gather.28
  303.3 57.6 all-gather.26
  691.1 72.4 reduce-scatter.7
  767.9 71.5 reduce-scatter.9
  843.2 72.1 reduce-scatter.11
  919.7 71.5 reduce-scatter.13
  995.3 125.2 reduce-scatter.15
  1125.2 126.0 reduce-scatter.17
  1255.2 126.0 reduce-scatter.19
where the time goes:
time: 1400 us; the launch traced here: 1390 us
  waiting for transfers between devices  687 us (49%)
  matrix products  346 us (25%)
  local copies, waits for them, and re-layouts  192 us (14%)
  other arithmetic  70.8 us (5%)
  blocking collectives  65.9 us (5%)
  between operations  18.4 us (1%)
    reduce_scatter x1, waiting for transfers between devices, per_device(): lax.psum_scatter(up_total, 'fsdp', scatter_dimension=0, tiled=True)  129 us
    reduce_scatter x1, waiting for transfers between devices, per_device(): lax.psum_scatter(down_total, 'fsdp', scatter_dimension=0, tiled=True)  128 us
    reduce_scatter x1, waiting for transfers between devices, per_device(): lax.psum_scatter(gate_total, 'fsdp', scatter_dimension=0, tiled=True)  128 us
    dot_general x36, matrix products, forward_product(): return jnp.dot(left, right, preferred_element_type=jnp.float32)  111 us
    dot_general x21, matrix products, outer_sum(): lax.dot_general(left, right, (((0,), (0,)), ((), ())), preferred_element_...  95.8 us
    reduce_scatter x1, waiting for transfers between devices, per_device(): lax.psum_scatter(output_total, 'fsdp', scatter_dimension=0, tiled=True)  74.3 us
    unnamed x2, blocking collectives  65.9 us
    all_gather x1, waiting for transfers between devices, per_device(): lax.all_gather(up_weight[0], 'fsdp', axis=0, tiled=True)  60 us
  transfers between devices with their start and end apart: 18, of which 11 were waited for; matrix products, arithmetic and copies ran while one was open for 24% of the time, Pallas kernels for 0%

commit v1 on v0

v1 whole, which is shorter than its diff:
```python
import functools
import math
import jax
import jax.numpy as jnp
from jax import lax
from jax.experimental import pallas as pl
from jax.experimental.pallas import tpu as pltpu
from jax.sharding import PartitionSpec as P

MESH = pl.DeviceIdType.MESH


def layout(n):
    rest=n//2
    R=min(4,rest); C=rest//R
    return R,C

def gather_kernel(n, P, *refs):
    ins=refs[:P]; outs=refs[P:2*P]; bufs=refs[2*P:3*P]
    own_sem,out_sem,s_zu,s_zd,s_yu,s_yd,s_sb,s_ex,r_main,r_sib=refs[3*P:]
    R,C=layout(n)
    sec=lax.axis_index("section"); f=lax.axis_index("fsdp")
    c=f%2; zy=f//2; y=zy%C; z=zy//C
    def dev(zz,yy,cc): return (sec,(zz*C+yy)*2+cc)
    bar=pltpu.get_barrier_semaphore()
    nb=[(z>0,(z-1,y,c)),(z<R-1,(z+1,y,c)),(y>0,(z,y-1,c)),(y<C-1,(z,y+1,c)),(c>=0,(z,y,1-c))]
    for p in range(P):
        pltpu.make_async_copy(ins[p],bufs[p].at[f],own_sem.at[p]).start()
    for cond,d in nb:
        @pl.when(cond)
        def _():
            pl.semaphore_signal(bar,1,device_id=dev(*d),device_id_type=MESH)
    pl.semaphore_wait(bar,sum(jnp.where(cond,1,0) for cond,d in nb))
    pending=[]
    def send(cond,p,zb,yb,target,ssem,rsem):
        blk=(zb*C+yb)*2+c
        k=zb*C+yb
        def mk():
            return pltpu.make_async_remote_copy(bufs[p].at[blk],bufs[p].at[blk],ssem.at[p,k],rsem.at[p,k],device_id=dev(*target),device_id_type=MESH)
        @pl.when(cond)
        def _(): mk().start()
        pending.append((cond,mk))
    def wait_main(cond,p,zb,yb):
        blk=(zb*C+yb)*2+c; k=zb*C+yb
        @pl.when(cond)
        def _():
            pltpu.make_async_remote_copy(bufs[p].at[blk],bufs[p].at[blk],s_sb.at[p,k],r_main.at[p,k],device_id=dev(z,y,1-c),device_id_type=MESH).wait_recv()
    offload = (C==2)
    T=(c>=0)
    def own(p):
        pltpu.make_async_copy(ins[p],bufs[p].at[f],own_sem.at[p]).wait()
        send(y>0,p,z,y,(z,y-1,c),s_yd,r_main)
        send(y<C-1,p,z,y,(z,y+1,c),s_yu,r_main)
        send(z>0,p,z,y,(z-1,y,c),s_zd,r_main)
        send(z<R-1,p,z,y,(z+1,y,c),s_zu,r_main)
        send(T,p,z,y,(z,y,1-c),s_sb,r_sib)
    def z_arrivals(p):
        for d in range(1,R):
            for sign in (-1,1):
                zb=z+sign*d
                ok=(zb>=0)&(zb<R)
                zbc=jnp.clip(zb,0,R-1)
                wait_main(ok,p,zbc,y)
                if sign<0:
                    send(ok&(z<R-1),p,zbc,y,(z+1,y,c),s_zu,r_main)
                else:
                    send(ok&(z>0),p,zbc,y,(z-1,y,c),s_zd,r_main)
                ydo=ok
                if offload: ydo=ok & jnp.logical_not((c==1)&(zbc==(z+1-2*(z%2))))
                send(ydo&(y>0),p,zbc,y,(z,y-1,c),s_yd,r_main)
                send(ydo&(y<C-1),p,zbc,y,(z,y+1,c),s_yu,r_main)
                send(ok,p,zbc,y,(z,y,1-c),s_sb,r_sib)
    def y_arrivals(p, near):
        for dy in range(1,C):
            for sign in (-1,1):
                yb=y+sign*dy
                oky=(yb>=0)&(yb<C)
                ybc=jnp.clip(yb,0,C-1)
                for d in ([0] if near else range(1,R)):
                    for zs in ((0,) if d==0 else (-1,1)):
                        zb=z+zs*d
                        ok=oky&(zb>=0)&(zb<R)
                        zbc=jnp.clip(zb,0,R-1)
                        wait_main(ok,p,zbc,ybc)
                        if C>2:
                            if sign<0: send(ok&(y<C-1),p,zbc,ybc,(z,y+1,c),s_yu,r_main)
                            else: send(ok&(y>0),p,zbc,ybc,(z,y-1,c),s_yd,r_main)
                        if offload and d==0:
                            send(ok&(c==1),p,zbc,ybc,(z+1-2*(z%2),y,c),s_ex,r_main)
                        send(ok,p,zbc,ybc,(z,y,1-c),s_sb,r_sib)
    def finish(p):
        def body(k,_):
            blk=k*2+1-c
            pltpu.make_async_remote_copy(bufs[p].at[blk],bufs[p].at[blk],s_sb.at[p,k],r_sib.at[p,k],device_id=dev(z,y,1-c),device_id_type=MESH).wait_recv()
            return 0
        lax.fori_loop(0,n//2,body,0)
        pltpu.make_async_copy(bufs[p],outs[p],out_sem.at[p]).start()
    LA=2
    for p in range(min(LA,P)): own(p)
    for p in range(P+2):
        if p+LA<P: own(p+LA)
        if p<P: z_arrivals(p)
        if 0<=p-1<P: y_arrivals(p-1,True)
        if 0<=p-2<P:
            y_arrivals(p-2,False)
            finish(p-2)
    for cond,mk in pending:
        @pl.when(cond)
        def _(): mk().wait_send()
    for p in range(P):
        pltpu.make_async_copy(bufs[p],outs[p],out_sem.at[p]).wait()

def gather(n, shards, cid=0):
    P=len(shards)
    R,C=layout(n)
    h=n//2
    D=pltpu.SemaphoreType.DMA
    return pl.pallas_call(functools.partial(gather_kernel,n,P),
        out_shape=[jax.ShapeDtypeStruct((n,)+s.shape,s.dtype) for s in shards],
        in_specs=[pl.BlockSpec(memory_space=pltpu.HBM)]*P,
        out_specs=[pl.BlockSpec(memory_space=pltpu.HBM)]*P,
        scratch_shapes=[pltpu.VMEM((n,)+s.shape,s.dtype) for s in shards]+[D((P,)),D((P,))]+[D((P,h))]*8,
        compiler_params=pltpu.CompilerParams(collective_id=cid,has_side_effects=True,vmem_limit_bytes=60<<20),
    )(*shards)

HEADS=8; HD=128; MQB=64; MEMK=128; EPS=1e-06; MASKED=-1e30

def nn(a,b): return jnp.dot(a,b,preferred_element_type=jnp.float32)
def nt(a,b): return lax.dot_general(a,b,(((1,),(1,)),((),())),preferred_element_type=jnp.float32)
def tn(a,b): return lax.dot_general(a,b,(((0,),(0,)),((),())),preferred_element_type=jnp.float32)

def chain_kernel(n, micro, T, D, FF, CACHE, NBLK, *refs):
    it=iter(refs)
    take=lambda k:[next(it) for _ in range(k)]
    x_hbm,og_hbm,docs,mk_hbm,mv_hbm,midx,mreset,gparts=take(8)
    wh=take(7)
    (so_hbm,ig_hbm,gsum,e_h,normed_h,mixed_h,n2_h,hidden_h,gi_h,ui_h,ai_h,dq_h,dk_h,dv_h)=take(14)
    W=take(7)
    (cur,eg,normed,q,k,v,mixed,n2,g,u,hidden,middle,p,rk,rv,grads,mxg,mg,acc,so,ig,mask,gain)=take(23)
    (w_sem,in_sem,c_sem,out_sem,xs,xr,gsems,grs)=take(8)
    Wq,Wk,Wv,Wo,Wg,Wu,Wd=W
    sec=lax.axis_index("section"); f=lax.axis_index("fsdp")
    scale=HD**-0.5
    B16=jnp.bfloat16
    bar=pltpu.get_barrier_semaphore()
    pl.semaphore_signal(bar,1,device_id=(1-sec,f),device_id_type=MESH)
    def load_cur(): return pltpu.make_async_copy(x_hbm,cur,in_sem.at[0])
    def load_eg(): return pltpu.make_async_copy(og_hbm,eg,in_sem.at[0])
    @pl.when(sec==0)
    def _(): load_cur().start()
    def load_cache(m,kv):
        src=(mk_hbm,mv_hbm)[kv]
        return [pltpu.make_async_copy(src.at[m,pl.ds(i*(CACHE//2),CACHE//2)],grads.at[2*kv+i],c_sem.at[2*kv+i]) for i in range(2)]
    @pl.when(sec==1)
    def _():
        for kv in range(2):
            for cp in load_cache(0,kv): cp.start()
        load_eg().start()
    for i in range(7): pltpu.make_async_copy(wh[i],W[i],w_sem.at[i]).start()
    def wait_w(t,*ids):
        @pl.when(t==0)
        def _():
            for i in ids: pltpu.make_async_copy(wh[i],W[i],w_sem.at[i]).wait()
    gain[...]=jnp.sum(gparts[...].astype(jnp.float32),axis=0)[0:8]
    gsum[...]=jnp.zeros_like(gsum)
    ri=lax.broadcasted_iota(jnp.int32,(T,T),0); ci=lax.broadcasted_iota(jnp.int32,(T,T),1)
    for m in range(micro):
        row=jnp.broadcast_to(docs[m:m+1,:].astype(jnp.float32),(T,T))
        mask[m]=jnp.where((row==row.T)&(ci<=ri),1.0,0.0)
    @pl.when(sec==0)
    def _():
        def z(i,_):
            o=pl.ds(pl.multiple_of(i*MEMK,MEMK),MEMK)
            for m in range(micro):
                rk[m,o,:]=jnp.zeros((MEMK,D),B16); rv[m,o,:]=jnp.zeros((MEMK,D),B16)
            return 0
        lax.fori_loop(0,NBLK,z,0)
        load_cur().wait()
    @pl.when(sec==1)
    def _():
        for m in range(micro):
            for kv in range(2):
                for cp in load_cache(m,kv): cp.wait()
                dst=(rk,rv)[kv]
                def body(b,_,m=m,kv=kv,dst=dst):
                    idx=midx[m,pl.ds(b,1),:]
                    col=jnp.broadcast_to(idx.astype(jnp.float32),(MEMK,MEMK)).T[:,0:1].astype(jnp.int32)
                    half=CACHE//2
                    io=lax.broadcasted_iota(jnp.int32,(MEMK,half),1)
                    tot=None
                    for i in range(2):
                        hot=jnp.where(io+i*half==col,1.0,0.0).astype(B16)
                        r=nn(hot,grads[2*kv+i])
                        tot = r if tot is None else tot + r
                    dst[m,pl.ds(pl.multiple_of(b*MEMK,MEMK),MEMK),:]=tot.astype(B16)
                    return 0
                lax.fori_loop(0,NBLK,body,0)
                if m+1<micro:
                    for cp in load_cache(m+1,kv): cp.start()
        load_eg().wait()
    pl.semaphore_wait(bar,1)
    def save(j,src,dst,m):
        return pltpu.make_async_copy(src.at[m],dst.at[m],out_sem.at[j,m])
    def xcopy(kind,m):
        src,dst=((so,cur),(ig,eg))[kind]
        return pltpu.make_async_remote_copy(src.at[m],dst.at[m],xs.at[kind,m],xr.at[kind,m],device_id=(1-sec,f),device_id_type=MESH)
    RB=64
    def rows_loop(fn):
        def b(i,_):
            fn(pl.ds(pl.multiple_of(i*RB,RB),RB)); return 0
        lax.fori_loop(0,T//RB,b,0)
    def cols_loop(N,CH,fn):
        def b(i,_):
            fn(pl.ds(pl.multiple_of(i*CH,CH),CH)); return 0
        lax.fori_loop(0,N//CH,b,0)
    def normalize(x,row):
        inv=lax.rsqrt(jnp.mean(x*x,axis=-1,keepdims=True)+EPS)
        return x*inv*gain[row:row+1,:]
    def norm_back(x,c,row):
        inv=lax.rsqrt(jnp.mean(x*x,axis=-1,keepdims=True)+EPS)
        s=c*gain[row:row+1,:]
        gsum[row:row+1,:]+=jnp.sum(c*x*inv,axis=0,keepdims=True)
        return inv*s-x*(inv*inv*inv)*jnp.mean(s*x,axis=-1,keepdims=True)
    def forward(t,m):
        @pl.when(sec==1)
        def _(): xcopy(0,m).wait_recv()
        def f1(r): normed[m,r,:]=normalize(cur[m,r,:].astype(jnp.float32),0).astype(B16)
        rows_loop(f1)
        save(0,normed,normed_h,m).start()
        wait_w(t,0,1,2)
        def f2(cs):
            a=normed[m]
            q[m,:,cs]=nn(a,Wq[:,cs]).astype(B16)
            k[m,:,cs]=nn(a,Wk[:,cs]).astype(B16)
            v[m,:,cs]=nn(a,Wv[:,cs]).astype(B16)
        cols_loop(D,256,f2)
        def head(h,_):
            hs=pl.ds(pl.multiple_of(h*HD,HD),HD)
            qh=q[m,:,hs]; kh=k[m,:,hs]; vh=v[m,:,hs]
            s=jnp.where(mask[m]>0.5,nt(qh,kh)*scale,MASKED)
            sr=[]
            for b in range(NBLK):
                live=(mreset[m,b:b+1,:]==0)&(sec==1)
                x=nt(qh[b*MQB:(b+1)*MQB],rk[m,b*MEMK:(b+1)*MEMK,hs])*scale
                sr.append(jnp.where(jnp.broadcast_to(live,(MQB,MEMK)),x,MASKED))
            sr=jnp.concatenate(sr,axis=0)
            top=jnp.maximum(jnp.max(s,axis=-1,keepdims=True),jnp.max(sr,axis=-1,keepdims=True))
            es=jnp.exp(s-top); er=jnp.exp(sr-top)
            inv=1.0/(jnp.sum(es,axis=-1,keepdims=True)+jnp.sum(er,axis=-1,keepdims=True))
            ps=(es*inv).astype(B16); pr=(er*inv).astype(B16)
            p[m,h,:,0:T]=ps; p[m,h,:,T:T+MEMK]=pr
            mr=jnp.concatenate([nn(pr[b*MQB:(b+1)*MQB],rv[m,b*MEMK:(b+1)*MEMK,hs]) for b in range(NBLK)],axis=0)
            mixed[m,:,hs]=(nn(ps,vh)+mr).astype(B16)
            return 0
        lax.fori_loop(0,HEADS,head,0)
        save(1,mixed,mixed_h,m).start()
        wait_w(t,3)
        def f3(cs): middle[m,:,cs]=cur[m,:,cs].astype(jnp.float32)+nn(mixed[m],Wo[:,cs])
        cols_loop(D,256,f3)
        def f4(r): n2[m,r,:]=normalize(middle[m,r,:],1).astype(B16)
        rows_loop(f4)
        save(2,n2,n2_h,m).start()
        wait_w(t,4,5)
        def f5(cs):
            a=n2[m]
            gg=nn(a,Wg[:,cs]); uu=nn(a,Wu[:,cs])
            g[m,:,cs]=gg.astype(B16); u[m,:,cs]=uu.astype(B16)
            hidden[m,:,cs]=(gg*jax.nn.sigmoid(gg)*uu).astype(B16)
        cols_loop(FF,256,f5)
        save(3,hidden,hidden_h,m).start()
        wait_w(t,6)
        def f6(cs): so[m,:,cs]=(middle[m,:,cs]+nn(hidden[m],Wd[:,cs])).astype(B16)
        cols_loop(D,256,f6)
        @pl.when(sec==0)
        def _(): xcopy(0,m).start()
        save(4,so,so_hbm,m).start()
    def backward(t,m):
        @pl.when(sec==0)
        def _(): xcopy(1,m).wait_recv()
        save(5,eg,e_h,m).start()
        def b1(cs):
            hg=nt(eg[m],Wd[cs,:])
            gg=g[m,:,cs].astype(jnp.float32); uu=u[m,:,cs].astype(jnp.float32)
            sg=jax.nn.sigmoid(gg)
            u[m,:,cs]=(hg*gg*sg).astype(B16)
            g[m,:,cs]=(hg*uu*sg*(1.0+gg*(1.0-sg))).astype(B16)
        cols_loop(FF,256,b1)
        save(6,g,gi_h,m).start(); save(7,u,ui_h,m).start()
        def b2(cs): acc[:,cs]=nt(g[m],Wg[cs,:])+nt(u[m],Wu[cs,:])
        cols_loop(D,256,b2)
        def b3(r):
            t_=eg[m,r,:].astype(jnp.float32)+norm_back(middle[m,r,:],acc[r,:],1)
            mg[r,:]=t_; grads[0,pl.ds(m*T+r.start,RB),:]=t_.astype(B16)
        rows_loop(b3)
        ms=pl.ds(pl.multiple_of(m*T,T),T)
        def gsave(j,i,dst): return pltpu.make_async_copy(grads.at[i,ms],dst.at[m],out_sem.at[j,m])
        gsave(8,0,ai_h).start()
        def b4(cs): mxg[:,cs]=nt(grads[0,ms,:],Wo[cs,:]).astype(B16)
        cols_loop(D,256,b4)
        def head(h,_):
            hs=pl.ds(pl.multiple_of(h*HD,HD),HD)
            qh=q[m,:,hs]; kh=k[m,:,hs]; vh=v[m,:,hs]; mh=mxg[:,hs]
            ps=p[m,h,:,0:T]; pr=p[m,h,:,T:T+MEMK]
            grads[3,ms,hs]=tn(ps,mh).astype(B16)
            pg=nt(mh,vh)
            rg=jnp.concatenate([nt(mh[b*MQB:(b+1)*MQB],rv[m,b*MEMK:(b+1)*MEMK,hs]) for b in range(NBLK)],axis=0)
            pf=ps.astype(jnp.float32); rf=pr.astype(jnp.float32)
            w=jnp.sum(pf*pg,axis=-1,keepdims=True)+jnp.sum(rf*rg,axis=-1,keepdims=True)
            ds=(pf*(pg-w)).astype(B16); dr=(rf*(rg-w)).astype(B16)
            qr=jnp.concatenate([nn(dr[b*MQB:(b+1)*MQB],rk[m,b*MEMK:(b+1)*MEMK,hs]) for b in range(NBLK)],axis=0)
            grads[1,ms,hs]=((nn(ds,kh)+qr)*scale).astype(B16)
            grads[2,ms,hs]=(tn(ds,qh)*scale).astype(B16)
            return 0
        lax.fori_loop(0,HEADS,head,0)
        gsave(9,1,dq_h).start(); gsave(10,2,dk_h).start(); gsave(11,3,dv_h).start()
        def b5(cs): acc[:,cs]=nt(grads[1,ms,:],Wq[cs,:])+nt(grads[2,ms,:],Wk[cs,:])+nt(grads[3,ms,:],Wv[cs,:])
        cols_loop(D,256,b5)
        def b6(r): ig[m,r,:]=(mg[r,:]+norm_back(cur[m,r,:].astype(jnp.float32),acc[r,:],0)).astype(B16)
        rows_loop(b6)
        @pl.when(sec==1)
        def _(): xcopy(1,m).start()
        save(12,ig,ig_hbm,m).start()
    def tick(t,_):
        first=sec==0
        is_f=jnp.where(first,t<micro,t%2==0)
        m=jnp.where(first,lax.rem(t,micro),t//2)
        @pl.when(is_f)
        def _(): forward(t,m)
        @pl.when(jnp.logical_not(is_f))
        def _(): backward(t,m)
        return 0
    lax.fori_loop(0,2*micro,tick,0)
    for m in range(micro):
        @pl.when(sec==0)
        def _(): xcopy(0,m).wait_send()
        @pl.when(sec==1)
        def _(): xcopy(1,m).wait_send()
        for j,(s,d) in enumerate([(normed,normed_h),(mixed,mixed_h),(n2,n2_h),(hidden,hidden_h),(so,so_hbm),(eg,e_h),(g,gi_h),(u,ui_h)]):
            save(j,s,d,m).wait()
        for j,i,d in ((8,0,ai_h),(9,1,dq_h),(10,2,dk_h),(11,3,dv_h)):
            pltpu.make_async_copy(grads.at[i,pl.ds(m*T,T)],d.at[m],out_sem.at[j,m]).wait()
        save(12,ig,ig_hbm,m).wait()

def chain(n, x, og, docs, mk, mv, midx, mreset, gparts, weights, cid=2):
    micro,T,D=x.shape
    FF=weights[4].shape[1]
    CACHE=mk.shape[1]; NBLK=midx.shape[1]
    B=jnp.bfloat16; F=jnp.float32
    V=pltpu.VMEM
    act=(micro,T,D); fact=(micro,T,FF)
    S=jax.ShapeDtypeStruct
    outs=[S(act,B),S(act,B),S((8,D),F),S(act,B),S(act,B),S(act,B),S(act,B),S(fact,B),S(fact,B),S(fact,B),S(act,B),S(act,B),S(act,B),S(act,B)]
    scratch=[V(w.shape,B) for w in weights]
    scratch+=[V(act,B)]*8+[V(fact,B)]*3+[V(act,F),V((micro,HEADS,T,T+MEMK),B),V((micro,NBLK*MEMK,D),B),V((micro,NBLK*MEMK,D),B),V((4,micro*T,D),B),V((T,D),B),V((T,D),F),V((T,D),F),V(act,B),V(act,B),V((micro,T,T),F),V((8,D),F)]
    DM=pltpu.SemaphoreType.DMA
    scratch+=[DM((7,)),DM((2,)),DM((4,)),DM((13,micro)),DM((2,micro)),DM((2,micro)),DM((1,)),DM((1,))]
    HB=pl.BlockSpec(memory_space=pltpu.HBM); VB=pl.BlockSpec(memory_space=pltpu.VMEM)
    reset=jnp.broadcast_to(mreset[:,:,None],(micro,NBLK,MEMK))
    return pl.pallas_call(functools.partial(chain_kernel,n,micro,T,D,FF,CACHE,NBLK),
        out_shape=outs,
        in_specs=[HB,HB,VB,HB,HB,VB,VB,VB]+[HB]*7,
        out_specs=[HB,HB,VB]+[HB]*11,
        scratch_shapes=scratch,
        compiler_params=pltpu.CompilerParams(collective_id=cid,has_side_effects=True,vmem_limit_bytes=64<<20),
    )(x,og,docs,mk,mv,midx,reset,gparts,*weights)


COLS=1024
def plan(n, lhs_shapes, rhs_shapes, weights):
    pieces=[]
    for w,(l,r) in enumerate(weights):
        rows=lhs_shapes[l][1]//n; N=rhs_shapes[r][1]
        step=512 if rows>64*16//n else 1024
        for c0 in range(0,N,step):
            pieces.append((w,rows,c0,min(step,N-c0)))
    return pieces

def reduce_kernel(n, tok, lhs_shapes, rhs_shapes, weights, pieces, vec_rows, SLOTS, *refs):
    NP=len(pieces); NL=len(lhs_shapes); NR=len(rhs_shapes); NW=len(weights)
    R,C=layout(n); H=n//2
    it=iter(refs)
    take=lambda k:[next(it) for _ in range(k)]
    lhs=take(NL); rhs=take(NR); vec=next(it)
    outs=take(NW); vec_out=next(it)
    ring=next(it); tbuf=take(NL)
    keep=take(NP); sibr=take(NP); yr=take(NP); xr=take(NP); zu=take(NP); zd=take(NP); fin=take(NP)
    shapes=sorted({(p[1],p[3]) for p in pieces})
    stage_of=dict(zip(shapes,take(len(shapes))))
    vecb=next(it); vecr=next(it)
    (ld_sem,sib_s,sib_r,y_s,y_r,x_s,x_r,zu_s,zu_r,zd_s,zd_r,v_s,v_r,o_s)=take(14)
    sec=lax.axis_index("section"); f=lax.axis_index("fsdp")
    c=f%2; zy=f//2; y=zy%C; z=zy//C
    offload=(C==2 and R%2==0)
    zx=z+1-2*(z%2)
    def dev(zz,yy,cc): return (sec,(zz*C+yy)*2+cc)
    def rcopy(src,dst,ss,rs,d):
        return pltpu.make_async_remote_copy(src,dst,ss,rs,device_id=dev(*d),device_id_type=MESH)
    LOGN=n.bit_length()-1
    nb=[]
    nb.append((c>=0,dev(z,y,1-c)))
    for k in range(1,C): nb.append((c>=0,dev(z,lax.rem(y+k,C),c)))
    nb.append((z>0,dev(z-1,y,c))); nb.append((z<R-1,dev(z+1,y,c)))
    for k in range(1,R.bit_length()-1): nb.append((c>=0,(sec,f^(2*C<<k))))
    bar=pltpu.get_barrier_semaphore()
    loads=[]
    def parts(ref,shape):
        return [(ref,c0,min(COLS,shape[1]-c0)) for c0 in range(0,shape[1],COLS)]
    load_id={}
    def need(kind,i):
        key=(kind,i)
        if key in load_id: return
        ref=lhs[i] if kind=="l" else rhs[i]
        sh=lhs_shapes[i] if kind=="l" else rhs_shapes[i]
        ids=[]
        for pr in parts(ref,sh):
            ids.append(len(loads)); loads.append(pr)
        load_id[key]=ids
    for l,r in weights:
        need("l",l); need("r",r)
    issued=[0]; freed=set()
    def load_copy(k):
        ref,c0,w=loads[k]
        return pltpu.make_async_copy(ref.at[:,pl.ds(c0,w)],ring.at[k%SLOTS,:,pl.ds(0,w)],ld_sem.at[k%SLOTS])
    def pump():
        while issued[0]<len(loads) and (issued[0]<SLOTS or (issued[0]-SLOTS) in freed):
            load_copy(issued[0]).start(); issued[0]+=1
    pump()
    for cond,d in nb:
        @pl.when(cond)
        def _(): pl.semaphore_signal(bar,1,device_id=d,device_id_type=MESH)
    waited=set()
    def wait_load(k):
        if k not in waited:
            load_copy(k).wait(); waited.add(k)
    transposed=set()
    def ensure_lhs(l):
        if l in transposed: return
        transposed.add(l)
        for j,k in enumerate(load_id[("l",l)]):
            wait_load(k)
            w=loads[k][2]
            CH=256
            def body(i,_,k=k,j=j):
                o=pl.multiple_of(i*CH,CH)
                tbuf[l][pl.ds(pl.multiple_of(j*COLS+o,CH),CH),:]=ring[k%SLOTS,:,pl.ds(o,CH)].T
                return 0
            lax.fori_loop(0,w//CH,body,0)
            freed.add(k)
        pump()
    last_use={}
    for i,(w,rows,c0,nc) in enumerate(pieces):
        l,r=weights[w]
        last_use[load_id[("r",r)][c0//COLS]]=i
    sends=[]
    stage_use={}
    def compute(i):
        w,rows,c0,nc=pieces[i]
        l,r=weights[w]
        ensure_lhs(l)
        k=load_id[("r",r)][c0//COLS]
        wait_load(k)
        lc=c0%COLS
        st=stage_of[(rows,nc)]
        u=stage_use.get((rows,nc),0); stage_use[(rows,nc)]=u+1
        slot=u%2
        if u>=2: sib_waits[(rows,nc)].pop(0)()
        T4=tbuf[l].reshape(H,2,rows,tok)
        CH=256
        for which,dst in ((1-c,st.at[slot]),(c,keep[i])):
            def body(j,_,which=which,dst=dst):
                o=pl.multiple_of(j*CH,CH)
                a=T4[:,which].reshape(H*rows,tok)
                b=ring[k%SLOTS,:,pl.ds(pl.multiple_of(lc+o,CH),CH)]
                res=jnp.dot(a,b,preferred_element_type=jnp.float32).astype(jnp.bfloat16)
                dst[:,:,pl.ds(o,CH)]=res.reshape(H,rows,CH)
                return 0
            lax.fori_loop(0,nc//CH,body,0)
            if dst is not keep[i]:
                cp=rcopy(st.at[slot],sibr[i],sib_s.at[i],sib_r.at[i],(z,y,1-c))
                cp.start()
                sib_waits.setdefault((rows,nc),[]).append(cp.wait_send)
        if last_use[k]==i:
            freed.add(k); pump()
    sib_waits={}
    def add_into(dst,src,rows):
        def body(j,_):
            o=pl.multiple_of(j*16,16)
            dst[pl.ds(o,16),:]=dst[pl.ds(o,16),:]+src[pl.ds(o,16),:]
            return 0
        lax.fori_loop(0,rows//16,body,0)
    def send(cond,cp):
        if cond is None: cp().start()
        else:
            @pl.when(cond)
            def _(): cp().start()
        sends.append((cond,cp))
    def sib_add(i):
        w,rows,c0,nc=pieces[i]
        rcopy(sibr[i],sibr[i],sib_s.at[i],sib_r.at[i],(z,y,1-c)).wait_recv()
        def body(k,_):
            add_into(keep[i].at[k],sibr[i].at[k],rows)
            return 0
        lax.fori_loop(0,H,body,0)
        if offload:
            send(c==1,lambda: rcopy(keep[i].at[zx*C+1-y],xr[i],x_s.at[i],x_r.at[i],(zx,y,c)))
        for kz in range(R-1,-1,-1):
            zt=lax.rem(z+kz,R)
            for ky in range(1,C):
                yt=lax.rem(y+ky,C)
                slot=C-1-ky
                cp=lambda zt=zt,yt=yt,slot=slot: rcopy(keep[i].at[zt*C+yt],yr[i].at[slot,zt],y_s.at[i,slot,zt],y_r.at[i,slot,zt],(z,yt,c))
                if offload and kz==0:
                    continue
                send((jnp.logical_not((c==1)&(zt==zx))) if offload else None,cp)
    def x_add(i):
        w,rows,c0,nc=pieces[i]
        if not offload: return
        @pl.when(c==1)
        def _():
            rcopy(xr[i],xr[i],x_s.at[i],x_r.at[i],(zx,y,c)).wait_recv()
            add_into(keep[i].at[z*C+1-y],xr[i],rows)
        send(None,lambda: rcopy(keep[i].at[z*C+1-y],yr[i].at[0,z],y_s.at[i,0,z],y_r.at[i,0,z],(z,1-y,c)))
    def y_add(i):
        w,rows,c0,nc=pieces[i]
        for kz in range(R-1,-1,-1):
            zt=lax.rem(z+kz,R)
            for slot in range(C-1):
                def go(zt=zt,slot=slot):
                    rcopy(yr[i].at[slot,zt],yr[i].at[slot,zt],y_s.at[i,slot,zt],y_r.at[i,slot,zt],(z,y,1-c)).wait_recv()
                    add_into(keep[i].at[zt*C+y],yr[i].at[slot,zt],rows)
                if offload and kz!=0:
                    pl.when(jnp.logical_not((c==1)&(zt==zx)))(go)
                else: go()
    def z_step(i,s):
        w,rows,c0,nc=pieces[i]
        def line(zs,up):
            rb,rr,ss=(zu,zu_r,zu_s) if up else (zd,zd_r,zd_s)
            first=(zs==0) if up else (zs==R-1)
            targets=range(R-1,zs,-1) if up else range(0,zs)
            nxt=zs+1 if up else zs-1
            cps=[]
            for t in targets:
                k=abs(t-zs)
                cps.append((k,lambda t=t,k=k: rcopy(keep[i].at[t*C+y],rb[i].at[k-1],ss.at[i,k-1],rr.at[i,k-1],(nxt,y,c)),t))
            def go():
                for k,cp,t in cps:
                    if not first:
                        rcopy(rb[i].at[k],rb[i].at[k],ss.at[i,k],rr.at[i,k],(zs,y,1-c)).wait_recv()
                        add_into(keep[i].at[t*C+y],rb[i].at[k],rows)
                    cp().start()
            pl.when(z==zs)(go)
            for k,cp,t in cps: sends.append((z==zs,cp))
        line(s,True)
        line(R-1-s,False)
    def final(i):
        w,rows,c0,nc=pieces[i]
        blk=z*C+y
        @pl.when(z>0)
        def _():
            rcopy(zu[i].at[0],zu[i].at[0],zu_s.at[i,0],zu_r.at[i,0],(z,y,1-c)).wait_recv()
        @pl.when(z<R-1)
        def _():
            rcopy(zd[i].at[0],zd[i].at[0],zd_s.at[i,0],zd_r.at[i,0],(z,y,1-c)).wait_recv()
        def body(j,_):
            o=pl.ds(pl.multiple_of(j*16,16),16)
            a=keep[i][blk,o,:].astype(jnp.float32)
            a=a+jnp.where(z>0,zu[i][0,o,:].astype(jnp.float32),0.0)+jnp.where(z<R-1,zd[i][0,o,:].astype(jnp.float32),0.0)
            fin[i][o,:]=a.astype(jnp.bfloat16)
            return 0
        lax.fori_loop(0,rows//16,body,0)
        pltpu.make_async_copy(fin[i],outs[w].at[:,pl.ds(c0,nc)],o_s.at[i]).start()
    def vec_step(k):
        if k>0:
            vcopy(k-1).wait()
            vecb[k]=vecb[k-1]+vecr[k-1]
        if k<LOGN: vcopy(k).start()
        else:
            cp=pltpu.make_async_copy(vecb.at[LOGN],vec_out,o_s.at[NP]); cp.start()
    def vcopy(k):
        return pltpu.make_async_remote_copy(vecb.at[k],vecr.at[k],v_s.at[k],v_r.at[k],device_id=(sec,f^(1<<k)),device_id_type=MESH)
    cp=pltpu.make_async_copy(vec,vecb.at[0],o_s.at[NP]); cp.start(); cp.wait()
    pl.semaphore_wait(bar,sum(jnp.where(cond,1,0) for cond,d in nb))
    LAGY=3
    for t in range(NP+LAGY+R+1):
        if t<NP: compute(t)
        if 0<=t-1<NP: sib_add(t-1)
        if 0<=t-2<NP: x_add(t-2)
        if t<=LOGN: vec_step(t)
        if 0<=t-LAGY<NP: y_add(t-LAGY)
        for s in range(R):
            i=t-LAGY-s
            if 0<=i<NP: z_step(i,s)
        i=t-LAGY-R
        if 0<=i<NP: final(i)
    for q in sib_waits.values():
        for wfn in q: wfn()
    for cond,cp in sends:
        if cond is None: cp().wait_send()
        else:
            @pl.when(cond)
            def _(): cp().wait_send()
    for i in range(NP):
        w,rows,c0,nc=pieces[i]
        pltpu.make_async_copy(fin[i],outs[w].at[:,pl.ds(c0,nc)],o_s.at[i]).wait()
    pltpu.make_async_copy(vecb.at[LOGN],vec_out,o_s.at[NP]).wait()

def reduce(n, lhs, rhs, weights, vec, cid=1, SLOTS=6):
    tok=lhs[0].shape[0]
    ls=[a.shape for a in lhs]; rs=[a.shape for a in rhs]
    pieces=plan(n,ls,rs,weights)
    R,C=layout(n); H=n//2
    NP=len(pieces)
    LOGN=n.bit_length()-1
    D=pltpu.SemaphoreType.DMA
    B=jnp.bfloat16
    V=pltpu.VMEM
    shapes=sorted({(p[1],p[3]) for p in pieces})
    scratch=[V((SLOTS,tok,COLS),B)]+[V((s[1],tok),B) for s in ls]
    scratch+=[V((H,p[1],p[3]),B) for p in pieces]
    scratch+=[V((H,p[1],p[3]),B) for p in pieces]
    scratch+=[V((C-1,R,p[1],p[3]),B) for p in pieces]
    scratch+=[V((p[1],p[3]) if C==2 else (16,128),B) for p in pieces]
    scratch+=[V((R-1,p[1],p[3]),B) for p in pieces]*2
    scratch+=[V((p[1],p[3]),B) for p in pieces]
    scratch+=[V((2,H)+s,B) for s in shapes]
    scratch+=[V((LOGN+1,)+vec.shape,vec.dtype),V((LOGN,)+vec.shape,vec.dtype)]
    scratch+=[D((SLOTS,)),D((NP,)),D((NP,)),D((NP,C-1,R)),D((NP,C-1,R)),D((NP,)),D((NP,)),D((NP,R-1)),D((NP,R-1)),D((NP,R-1)),D((NP,R-1)),D((LOGN,)),D((LOGN,)),D((NP+1,))]
    HB=pl.BlockSpec(memory_space=pltpu.HBM)
    res=pl.pallas_call(functools.partial(reduce_kernel,n,tok,ls,rs,weights,pieces,vec.shape[0],SLOTS),
        out_shape=[jax.ShapeDtypeStruct((ls[l][1]//n,rs[r][1]),B) for l,r in weights]+[jax.ShapeDtypeStruct(vec.shape,vec.dtype)],
        in_specs=[HB]*(len(lhs)+len(rhs)+1),
        out_specs=[HB]*(len(weights)+1),
        scratch_shapes=scratch,
        compiler_params=pltpu.CompilerParams(collective_id=cid,has_side_effects=True,vmem_limit_bytes=63<<20),
    )(*lhs,*rhs,vec)
    return res[:-1],res[-1]


def per_device(
    block_input, output_grad, document_ids, memory_keys, memory_values, memory_index, memory_reset,
    query_weight, key_weight, value_weight, output_weight, gate_weight, up_weight, down_weight,
    attend_gain, feed_gain,
):
    n = lax.axis_size("fsdp")
    f = lax.axis_index("fsdp")
    micro, T, D = block_input.shape
    FF = gate_weight.shape[2]
    gw = attend_gain.shape[1]
    vec = jnp.zeros((16, D), jnp.bfloat16)
    vec = lax.dynamic_update_slice(vec, jnp.concatenate([attend_gain, feed_gain]), (0, f * gw))
    shards = [w[0] for w in (query_weight, key_weight, value_weight, output_weight, gate_weight, up_weight, down_weight)]
    rows = [s.shape[0] for s in shards]
    padded = [jnp.pad(s, ((0, -s.shape[0] % 16), (0, 0))) for s in shards]
    gathered = gather(n, [vec] + padded, 0)
    weights = [g[:, :r].reshape(n * r, g.shape[2]) for g, r in zip(gathered[1:], rows)]
    (so, ig, gsum, e, normed, mixed, n2, hidden, gi, ui, ai, dq, dk, dv) = chain(
        n, block_input, output_grad, document_ids, memory_keys, memory_values, memory_index, memory_reset, gathered[0], weights, 2)
    flat = lambda a: a.reshape(micro * T, a.shape[2])
    hid = flat(hidden)
    rd = rows[6]
    if rd % 16:
        hid = jnp.pad(hid.reshape(micro * T, n, rd), ((0, 0), (0, 0), (0, -rd % 16))).reshape(micro * T, -1)
    lhs = [hid, flat(n2), flat(mixed), flat(normed)]
    rhs = [flat(a) for a in (e, gi, ui, ai, dv, dk, dq)]
    order = [(0, 0), (1, 1), (1, 2), (2, 3), (3, 4), (3, 5), (3, 6)]
    sums, total = reduce(n, lhs, rhs, order, gsum, 1)
    gd, gg, gu, go, gv, gk, gq = sums
    gains = lax.dynamic_slice(total, (0, f * gw), (2, gw)).astype(jnp.bfloat16)
    return (so[None], ig[None], gq[None], gk[None], gv[None], go[None], gg[None], gu[None], gd[:rd][None], gains[0:1], gains[1:2])


def solution(mesh):
    w = P("section", "fsdp", None)
    r = P(None, "fsdp", None)
    v = P("section", "fsdp")
    return jax.shard_map(
        per_device,
        mesh=mesh,
        in_specs=(r, r, P(None, "fsdp"), r, r, r, P(None, "fsdp")) + (w,) * 7 + (v, v),
        out_specs=(P("section", None, "fsdp", None),) * 2 + (w,) * 7 + (v, v),
        check_vma=False,
    )
```

time: 1400 us -> 452 us (0.32)
  waiting for transfers between devices: 687 us -> 0 us
  Pallas kernels: 0 us -> 438 us
  matrix products: 346 us -> 0 us
  local copies, waits for them, and re-layouts: 192 us -> 13 us
  other arithmetic: 70.8 us -> 0.68 us
  blocking collectives: 65.9 us -> 0 us
  between operations: 18.4 us -> 0.74 us
    reduce_scatter x7 -> x0, waiting for transfers between devices: 479 us -> none  [the longest x1 129 us: per_device(): lax.psum_scatter(up_total, 'fsdp', scatter_dimension=0, tiled=True)]
    pallas_call x0 -> x3, Pallas kernels: none -> 438 us  [the longest x1 157 us: reduce(): pl.pallas_call(functools.partial(reduce_kernel, n, tok, ls, rs, weights,...]
    dot_general x120 -> x0, matrix products: 346 us -> none  [the longest x36 111 us: forward_product(): return jnp.dot(left, right, preferred_element_type=jnp.float32)]
    all_gather x7 -> x0, waiting for transfers between devices: 195 us -> none  [the longest x1 60 us: per_device(): lax.all_gather(up_weight[0], 'fsdp', axis=0, tiled=True)]
    unnamed x2 -> x0, blocking collectives: 65.9 us -> none
    gather x12 -> x0, local copies, waits for them, and re-layouts: 61.6 us -> none  [the longest x6 31.4 us: recall(): jnp.take(keys_here, flat, axis=0)]
    reshape x36 -> x0, local copies, waits for them, and re-layouts: 45.3 us -> none  [the longest x6 12.9 us: layer_forward(): mixed = mixed + jnp.einsum('hbqk,bkhd->bqhd', recalled_prob.astype(jnp.bf...]
    unnamed x392 -> x25, local copies, waits for them, and re-layouts: 49.5 us -> 10.1 us
  transfers between devices with their start and end apart: 18 -> 0, of which waited for: 11 -> 0; matrix products, arithmetic and copies ran while one was open for 24% -> 0% of each run, Pallas kernels for 0% -> 0%
where the time goes in v1:
time: 452 us
  Pallas kernels  438 us (97%)
  local copies, waits for them, and re-layouts  13 us (3%)
    pallas_call x1, Pallas kernels, reduce(): pl.pallas_call(functools.partial(reduce_kernel, n, tok, ls, rs, weights,...  157 us
    pallas_call x1, Pallas kernels, gather(): pl.pallas_call(functools.partial(gather_kernel, n, P), out_shape=[jax.Sha...  142 us
    pallas_call x1, Pallas kernels, chain(): pl.pallas_call(functools.partial(chain_kernel, n, micro, T, D, FF, CACHE,...  138 us
    unnamed x25, local copies, waits for them, and re-layouts  10.1 us

profile of v1, /device:TPU:0, one launch (start us, length us, event | category | flops | bytes accessed | tf_op | source)
XLA Modules:
  0.0 452.1 jit_solution(445299762110328416)
XLA Ops:
  0.6 0.7 pad_maximum_fusion
  1.3 1.3 broadcast_in_dim.36.refs_6_
  2.7 0.2 dynamic_update_slice.3.refs_0_
  2.9 0.0 copy-start.3
  2.9 0.6 copy-done.3
  3.5 142.1 %shard_map.239 = (bf16[16,16,1024]{2,1,0:T(8,128)(2,1)}, bf16[16,64,1024]{2,1,0:T(8,128)(2,1)}, bf16[16,64,1024]{2,1,0:T(8,128)(2,1)}, bf16[16,64,1024]{2,1,0:T(...) custom-call(bf16[16,1024]{1,0:T(8,128)(2,1)} %copy-done.3, ...), custom_call_target="tpu_custom_call" | custom-call | tf_op jit(solution)/shard_map/pallas_call | solution.py:118
  145.7 138.4 %shard_map.240 = (bf16[2,256,1024]{2,1,0:T(8,128)(2,1)}, bf16[2,256,1024]{2,1,0:T(8,128)(2,1)}, f32[8,1024]{1,0:T(8,128)}, bf16[2,256,1024]{2,1,0:T(8,128)(2,1)}...) custom-call(bf16[2,256,1024]{2,1,0:T(8,128)(2,1)} %refs_0_.1, ...), custom_call_target="tpu_custom_call" | custom-call | tf_op jit(solution)/shard_map/pallas_call | solution.py:359
  284.1 157.2 %shard_map.241 = (bf16[176,1024]{1,0:T(8,128)(2,1)}, bf16[64,2816]{1,0:T(8,128)(2,1)}, bf16[64,2816]{1,0:T(8,128)(2,1)}, bf16[64,1024]{1,0:T(8,128)(2,1)}, bf16[...) custom-call(bf16[512,2816]{1,0:T(8,128)(2,1)} %bitcast.37, ...), custom_call_target="tpu_custom_call" | custom-call | tf_op jit(solution)/shard_map/pallas_call | solution.py:629
  441.3 0.0 copy-start.7
  441.3 0.0 copy-start.6
  441.3 0.0 copy-start.5
  441.3 0.0 copy-start.4
  441.3 0.0 copy-start.2
  441.3 0.8 dynamic-slice_convert_fusion
  442.2 0.5 fusion
  442.7 0.0 copy-start.1
  442.7 0.0 copy-start
  442.7 2.3 copy.37
  445.0 2.3 copy.38
  447.3 0.0 copy-done.7
  447.3 0.7 copy.39
  447.9 0.0 copy-done.6
  447.9 0.7 copy.40
  448.6 0.0 copy-done.5
  448.6 0.7 copy.41
  449.3 0.0 copy-done.4
  449.3 0.7 copy.42
  449.9 0.0 copy-done.2
  449.9 0.7 copy.43
  450.7 0.0 copy-done.1
  450.7 0.7 copy.44
  451.4 0.0 copy-done
  451.4 0.7 copy.45
  (1 shorter events, 0.0 us)
Async XLA Ops:
  2.9 0.6 copy-start.3
  441.3 6.0 %copy-start.7 = (bf16[64,1024]{1,0:T(8,128)(2,1)S(1)}, bf16[64,1024]{1,0:T(8,128)(2,1)}, u32[]{:S(2)}) copy-start(bf16[64,1024]{1,0:T(8,128)(2,1)} %get-tuple-element.63) | copy-start | bytes 393220
  441.3 6.7 %copy-start.6 = (bf16[64,1024]{1,0:T(8,128)(2,1)S(1)}, bf16[64,1024]{1,0:T(8,128)(2,1)}, u32[]{:S(2)}) copy-start(bf16[64,1024]{1,0:T(8,128)(2,1)} %get-tuple-element.64) | copy-start | bytes 393220
  441.3 7.3 %copy-start.5 = (bf16[64,1024]{1,0:T(8,128)(2,1)S(1)}, bf16[64,1024]{1,0:T(8,128)(2,1)}, u32[]{:S(2)}) copy-start(bf16[64,1024]{1,0:T(8,128)(2,1)} %get-tuple-element.65) | copy-start | bytes 393220
  441.3 8.0 %copy-start.4 = (bf16[64,1024]{1,0:T(8,128)(2,1)S(1)}, bf16[64,1024]{1,0:T(8,128)(2,1)}, u32[]{:S(2)}) copy-start(bf16[64,1024]{1,0:T(8,128)(2,1)} %get-tuple-element.66) | copy-start | bytes 393220
  441.3 8.6 %copy-start.2 = (bf16[64,2816]{1,0:T(8,128)(2,1)S(1)}, bf16[64,2816]{1,0:T(8,128)(2,1)}, u32[]{:S(2)}) copy-start(bf16[64,2816]{1,0:T(8,128)(2,1)} %get-tuple-element.67) | copy-start | bytes 1081348
  442.7 8.0 %copy-start.1 = (bf16[64,2816]{1,0:T(8,128)(2,1)S(1)}, bf16[64,2816]{1,0:T(8,128)(2,1)}, u32[]{:S(2)}) copy-start(bf16[64,2816]{1,0:T(8,128)(2,1)} %get-tuple-element.68) | copy-start | bytes 1081348
  442.7 8.7 %copy-start = (bf16[176,1024]{1,0:T(8,128)(2,1)S(1)}, bf16[176,1024]{1,0:T(8,128)(2,1)}, u32[]{:S(2)}) copy-start(bf16[176,1024]{1,0:T(8,128)(2,1)} %get-tuple-element.69) | copy-start | bytes 1081348

commit v2 on v1

--- a/solution.py
+++ b/solution.py
@@ -124,86 +124,62 @@
     )(*shards)
 
 HEADS=8; HD=128; MQB=64; MEMK=128; EPS=1e-06; MASKED=-1e30
+XC=256
 
 def nn(a,b): return jnp.dot(a,b,preferred_element_type=jnp.float32)
 def nt(a,b): return lax.dot_general(a,b,(((1,),(1,)),((),())),preferred_element_type=jnp.float32)
 def tn(a,b): return lax.dot_general(a,b,(((0,),(0,)),((),())),preferred_element_type=jnp.float32)
 
-def chain_kernel(n, micro, T, D, FF, CACHE, NBLK, *refs):
+def front_kernel(n, fused, micro, T, D, FF, CACHE, NBLK, *refs):
     it=iter(refs)
     take=lambda k:[next(it) for _ in range(k)]
-    x_hbm,og_hbm,docs,mk_hbm,mv_hbm,midx,mreset,gparts=take(8)
-    wh=take(7)
+    x_hbm,og_hbm,docs,mk_hbm,mv_hbm,midx,mreset=take(7)
+    ins=take(8)
     (so_hbm,ig_hbm,gsum,e_h,normed_h,mixed_h,n2_h,hidden_h,gi_h,ui_h,ai_h,dq_h,dk_h,dv_h)=take(14)
-    W=take(7)
-    (cur,eg,normed,q,k,v,mixed,n2,g,u,hidden,middle,p,rk,rv,grads,mxg,mg,acc,so,ig,mask,gain)=take(23)
-    (w_sem,in_sem,c_sem,out_sem,xs,xr,gsems,grs)=take(8)
+    bufs=take(8)
+    (cur,eg,normed,q,k,v,mixed,n2,g,u,hidden,middle,p,rk,rv,grads,mg,acc,so,ig,mask,gain)=take(22)
+    (own_sem,in_sem,c_sem,out_sem,xs,xr,es,er)=take(8)
+    ag_sems=take(8)
+    B16=jnp.bfloat16
+    W=[b.reshape(b.shape[0]*b.shape[1],b.shape[2]) if fused else b for b in bufs[1:]]
     Wq,Wk,Wv,Wo,Wg,Wu,Wd=W
     sec=lax.axis_index("section"); f=lax.axis_index("fsdp")
     scale=HD**-0.5
-    B16=jnp.bfloat16
+    R,C=layout(n)
+    c=f%2; zy=f//2; y=zy%C; z=zy//C
+    def dev(d): return (sec,(d[0]*C+d[1])*2+d[2])
+    pieces=[(i,None) for i in range(7)]+[(7,j) for j in range(D//XC)]
+    NP=len(pieces)
+    nb=[(c>=0,(1-sec,f))]
+    if fused:
+        nb+=[(z>0,dev((z-1,y,c))),(z<R-1,dev((z+1,y,c))),(y>0,dev((z,y-1,c))),(y<C-1,dev((z,y+1,c))),(c>=0,dev((z,y,1-c)))]
     bar=pltpu.get_barrier_semaphore()
-    pl.semaphore_signal(bar,1,device_id=(1-sec,f),device_id_type=MESH)
+    for cond,d in nb:
+        @pl.when(cond)
+        def _(d=d): pl.semaphore_signal(bar,1,device_id=d,device_id_type=MESH)
+    def own_copy(i):
+        return pltpu.make_async_copy(ins[i],bufs[i].at[f] if fused else bufs[i],own_sem.at[i])
+    for i in range(8): own_copy(i).start()
     def load_cur(): return pltpu.make_async_copy(x_hbm,cur,in_sem.at[0])
     def load_eg(): return pltpu.make_async_copy(og_hbm,eg,in_sem.at[0])
+    HC=CACHE//2
+    def load_cache(m,kv):
+        src=(mk_hbm,mv_hbm)[kv]
+        return [pltpu.make_async_copy(src.at[m,pl.ds(i*HC,HC)],grads.at[2*kv+i],c_sem.at[2*kv+i]) for i in range(2)]
     @pl.when(sec==0)
     def _(): load_cur().start()
-    def load_cache(m,kv):
-        src=(mk_hbm,mv_hbm)[kv]
-        return [pltpu.make_async_copy(src.at[m,pl.ds(i*(CACHE//2),CACHE//2)],grads.at[2*kv+i],c_sem.at[2*kv+i]) for i in range(2)]
     @pl.when(sec==1)
     def _():
         for kv in range(2):
             for cp in load_cache(0,kv): cp.start()
         load_eg().start()
-    for i in range(7): pltpu.make_async_copy(wh[i],W[i],w_sem.at[i]).start()
-    def wait_w(t,*ids):
-        @pl.when(t==0)
-        def _():
-            for i in ids: pltpu.make_async_copy(wh[i],W[i],w_sem.at[i]).wait()
-    gain[...]=jnp.sum(gparts[...].astype(jnp.float32),axis=0)[0:8]
-    gsum[...]=jnp.zeros_like(gsum)
-    ri=lax.broadcasted_iota(jnp.int32,(T,T),0); ci=lax.broadcasted_iota(jnp.int32,(T,T),1)
-    for m in range(micro):
-        row=jnp.broadcast_to(docs[m:m+1,:].astype(jnp.float32),(T,T))
-        mask[m]=jnp.where((row==row.T)&(ci<=ri),1.0,0.0)
-    @pl.when(sec==0)
-    def _():
-        def z(i,_):
-            o=pl.ds(pl.multiple_of(i*MEMK,MEMK),MEMK)
-            for m in range(micro):
-                rk[m,o,:]=jnp.zeros((MEMK,D),B16); rv[m,o,:]=jnp.zeros((MEMK,D),B16)
-            return 0
-        lax.fori_loop(0,NBLK,z,0)
-        load_cur().wait()
-    @pl.when(sec==1)
-    def _():
-        for m in range(micro):
-            for kv in range(2):
-                for cp in load_cache(m,kv): cp.wait()
-                dst=(rk,rv)[kv]
-                def body(b,_,m=m,kv=kv,dst=dst):
-                    idx=midx[m,pl.ds(b,1),:]
-                    col=jnp.broadcast_to(idx.astype(jnp.float32),(MEMK,MEMK)).T[:,0:1].astype(jnp.int32)
-                    half=CACHE//2
-                    io=lax.broadcasted_iota(jnp.int32,(MEMK,half),1)
-                    tot=None
-                    for i in range(2):
-                        hot=jnp.where(io+i*half==col,1.0,0.0).astype(B16)
-                        r=nn(hot,grads[2*kv+i])
-                        tot = r if tot is None else tot + r
-                    dst[m,pl.ds(pl.multiple_of(b*MEMK,MEMK),MEMK),:]=tot.astype(B16)
-                    return 0
-                lax.fori_loop(0,NBLK,body,0)
-                if m+1<micro:
-                    for cp in load_cache(m+1,kv): cp.start()
-        load_eg().wait()
-    pl.semaphore_wait(bar,1)
     def save(j,src,dst,m):
         return pltpu.make_async_copy(src.at[m],dst.at[m],out_sem.at[j,m])
-    def xcopy(kind,m):
-        src,dst=((so,cur),(ig,eg))[kind]
-        return pltpu.make_async_remote_copy(src.at[m],dst.at[m],xs.at[kind,m],xr.at[kind,m],device_id=(1-sec,f),device_id_type=MESH)
+    def xcopy(m,j):
+        cs=pl.ds(j*XC,XC)
+        return pltpu.make_async_remote_copy(so.at[m,:,cs],cur.at[m,:,cs],xs.at[m,j],xr.at[m,j],device_id=(1-sec,f),device_id_type=MESH)
+    def ecopy(m):
+        return pltpu.make_async_remote_copy(ig.at[m],eg.at[m],es.at[m],er.at[m],device_id=(1-sec,f),device_id_type=MESH)
     RB=64
     def rows_loop(fn):
         def b(i,_):
@@ -212,55 +188,55 @@
     def cols_loop(N,CH,fn):
         def b(i,_):
             fn(pl.ds(pl.multiple_of(i*CH,CH),CH)); return 0
-        lax.fori_loop(0,N//CH,b,0)
+        lax.fori_loop(0,N//CH,b,0,unroll=N//CH)
     def normalize(x,row):
         inv=lax.rsqrt(jnp.mean(x*x,axis=-1,keepdims=True)+EPS)
         return x*inv*gain[row:row+1,:]
-    def norm_back(x,c,row):
+    def norm_back(x,cc,row):
         inv=lax.rsqrt(jnp.mean(x*x,axis=-1,keepdims=True)+EPS)
-        s=c*gain[row:row+1,:]
-        gsum[row:row+1,:]+=jnp.sum(c*x*inv,axis=0,keepdims=True)
+        s=cc*gain[row:row+1,:]
+        gsum[row:row+1,:]+=jnp.sum(cc*x*inv,axis=0,keepdims=True)
         return inv*s-x*(inv*inv*inv)*jnp.mean(s*x,axis=-1,keepdims=True)
-    def forward(t,m):
-        @pl.when(sec==1)
-        def _(): xcopy(0,m).wait_recv()
+    def f_norm(m):
         def f1(r): normed[m,r,:]=normalize(cur[m,r,:].astype(jnp.float32),0).astype(B16)
         rows_loop(f1)
         save(0,normed,normed_h,m).start()
-        wait_w(t,0,1,2)
-        def f2(cs):
-            a=normed[m]
-            q[m,:,cs]=nn(a,Wq[:,cs]).astype(B16)
-            k[m,:,cs]=nn(a,Wk[:,cs]).astype(B16)
-            v[m,:,cs]=nn(a,Wv[:,cs]).astype(B16)
+    def f_proj(m,dst,w):
+        def f2(cs): dst[m,:,cs]=nn(normed[m],w[:,cs]).astype(B16)
         cols_loop(D,256,f2)
+    def f_attend(m,recall):
         def head(h,_):
             hs=pl.ds(pl.multiple_of(h*HD,HD),HD)
             qh=q[m,:,hs]; kh=k[m,:,hs]; vh=v[m,:,hs]
-            s=jnp.where(mask[m]>0.5,nt(qh,kh)*scale,MASKED)
+            s=jnp.where(mask[m].astype(jnp.float32)>0.5,nt(qh,kh)*scale,MASKED)
+            if not recall:
+                es_=jnp.exp(s-jnp.max(s,axis=-1,keepdims=True))
+                ps=(es_*(1.0/jnp.sum(es_,axis=-1,keepdims=True))).astype(B16)
+                p[m,h,:,0:T]=ps
+                mixed[m,:,hs]=nn(ps,vh).astype(B16)
+                return 0
             sr=[]
             for b in range(NBLK):
-                live=(mreset[m,b:b+1,:]==0)&(sec==1)
                 x=nt(qh[b*MQB:(b+1)*MQB],rk[m,b*MEMK:(b+1)*MEMK,hs])*scale
-                sr.append(jnp.where(jnp.broadcast_to(live,(MQB,MEMK)),x,MASKED))
+                sr.append(jnp.where(jnp.broadcast_to(mreset[m,b:b+1,:]==0,(MQB,MEMK)),x,MASKED))
             sr=jnp.concatenate(sr,axis=0)
             top=jnp.maximum(jnp.max(s,axis=-1,keepdims=True),jnp.max(sr,axis=-1,keepdims=True))
-            es=jnp.exp(s-top); er=jnp.exp(sr-top)
-            inv=1.0/(jnp.sum(es,axis=-1,keepdims=True)+jnp.sum(er,axis=-1,keepdims=True))
-            ps=(es*inv).astype(B16); pr=(er*inv).astype(B16)
+            es_=jnp.exp(s-top); er_=jnp.exp(sr-top)
+            inv=1.0/(jnp.sum(es_,axis=-1,keepdims=True)+jnp.sum(er_,axis=-1,keepdims=True))
+            ps=(es_*inv).astype(B16); pr=(er_*inv).astype(B16)
             p[m,h,:,0:T]=ps; p[m,h,:,T:T+MEMK]=pr
             mr=jnp.concatenate([nn(pr[b*MQB:(b+1)*MQB],rv[m,b*MEMK:(b+1)*MEMK,hs]) for b in range(NBLK)],axis=0)
             mixed[m,:,hs]=(nn(ps,vh)+mr).astype(B16)
             return 0
-        lax.fori_loop(0,HEADS,head,0)
+        lax.fori_loop(0,HEADS,head,0,unroll=HEADS)
         save(1,mixed,mixed_h,m).start()
-        wait_w(t,3)
+    def f_out(m):
         def f3(cs): middle[m,:,cs]=cur[m,:,cs].astype(jnp.float32)+nn(mixed[m],Wo[:,cs])
         cols_loop(D,256,f3)
         def f4(r): n2[m,r,:]=normalize(middle[m,r,:],1).astype(B16)
         rows_loop(f4)
         save(2,n2,n2_h,m).start()
-        wait_w(t,4,5)
+    def f_gate(m):
         def f5(cs):
             a=n2[m]
             gg=nn(a,Wg[:,cs]); uu=nn(a,Wu[:,cs])
@@ -268,15 +244,173 @@
             hidden[m,:,cs]=(gg*jax.nn.sigmoid(gg)*uu).astype(B16)
         cols_loop(FF,256,f5)
         save(3,hidden,hidden_h,m).start()
-        wait_w(t,6)
-        def f6(cs): so[m,:,cs]=(middle[m,:,cs]+nn(hidden[m],Wd[:,cs])).astype(B16)
-        cols_loop(D,256,f6)
+    def f_down(m,j):
+        cs=pl.ds(j*XC,XC)
+        so[m,:,cs]=(middle[m,:,cs]+nn(hidden[m],Wd[:,cs])).astype(B16)
+    def recall(m,kv):
+        for cp in load_cache(m,kv): cp.wait()
+        dst=(rk,rv)[kv]
+        def body(b,_):
+            idx=midx[m,pl.ds(b,1),:]
+            col=jnp.broadcast_to(idx.astype(jnp.float32),(MEMK,MEMK)).T[:,0:1].astype(jnp.int32)
+            io=lax.broadcasted_iota(jnp.int32,(MEMK,HC),1)
+            rows=nn(jnp.where(io==col,1.0,0.0).astype(B16),grads[2*kv])
+            rows=rows+nn(jnp.where(io+HC==col,1.0,0.0).astype(B16),grads[2*kv+1])
+            dst[m,pl.ds(pl.multiple_of(b*MEMK,MEMK),MEMK),:]=rows.astype(B16)
+            return 0
+        lax.fori_loop(0,NBLK,body,0)
+        if m+1<micro:
+            for cp in load_cache(m+1,kv): cp.start()
+    def setup():
+        parts=bufs[0][...]
+        gain[...]=jnp.sum(parts.astype(jnp.float32),axis=0)[0:8]
+    def each(fn):
+        def b(m,_):
+            fn(m); return 0
+        return lambda: lax.fori_loop(0,micro,b,0)
+    def down(j):
+        def go():
+            def b(m,_):
+                f_down(m,j); xcopy(m,j).start(); return 0
+            lax.fori_loop(0,micro,b,0)
+        return go
+    first={0:[each(f_norm)],1:[each(lambda m:f_proj(m,q,Wq))],2:[each(lambda m:f_proj(m,k,Wk))],
+        3:[each(lambda m:f_proj(m,v,Wv)),lambda:f_attend(0,False)],
+        4:[lambda:[f_attend(m,False) for m in range(1,micro)],each(f_out)],
+        6:[each(f_gate)]}
+    for j in range(D//XC): first[7+j]=[down(j)]
+    units=[(m,kv) for m in range(micro) for kv in range(2)]
+    second={i:[functools.partial(recall,*un)] for i,un in enumerate(units)}
+    def arrived(i):
+        if i==0: setup()
         @pl.when(sec==0)
-        def _(): xcopy(0,m).start()
+        def _():
+            for fn in first.get(i,[]): fn()
+        @pl.when(sec==1)
+        def _():
+            for fn in second.get(i,[]): fn()
+    gsum[...]=jnp.zeros_like(gsum)
+    ri=lax.broadcasted_iota(jnp.int32,(T,T),0); ci=lax.broadcasted_iota(jnp.int32,(T,T),1)
+    def prepare():
+        for m in range(micro):
+            row=jnp.broadcast_to(docs[m:m+1,:].astype(jnp.float32),(T,T))
+            mask[m]=jnp.where((row==row.T)&(ci<=ri),1.0,0.0).astype(B16)
+        @pl.when(sec==0)
+        def _():
+            def zero(i,_):
+                o=pl.ds(pl.multiple_of(i*MEMK,MEMK),MEMK)
+                for m in range(micro):
+                    rk[m,o,:]=jnp.zeros((MEMK,D),B16); rv[m,o,:]=jnp.zeros((MEMK,D),B16)
+                return 0
+            lax.fori_loop(0,NBLK,zero,0)
+            def zero_p(h,_):
+                for m in range(micro): p[m,h,:,T:T+MEMK]=jnp.zeros((T,MEMK),B16)
+                return 0
+            lax.fori_loop(0,HEADS,zero_p,0)
+            load_cur().wait()
+        @pl.when(sec==1)
+        def _(): load_eg().wait()
+    pl.semaphore_wait(bar,sum(jnp.where(cond,1,0) for cond,d in nb))
+    pending=[]
+    if fused:
+        s_zu,s_zd,s_yu,s_yd,s_sb,s_ex,r_main,r_sib=ag_sems
+        def part(i,blk):
+            b,j=pieces[i]
+            return bufs[b].at[blk] if j is None else bufs[b].at[blk,:,pl.ds(j*XC,XC)]
+        def send(cond,i,zb,yb,target,ssem,rsem):
+            blk=(zb*C+yb)*2+c; kk=zb*C+yb
+            def mk():
+                return pltpu.make_async_remote_copy(part(i,blk),part(i,blk),ssem.at[i,kk],rsem.at[i,kk],device_id=dev(target),device_id_type=MESH)
+            @pl.when(cond)
+            def _(): mk().start()
+            pending.append((cond,mk))
+        def wait_main(cond,i,zb,yb):
+            blk=(zb*C+yb)*2+c; kk=zb*C+yb
+            @pl.when(cond)
+            def _():
+                pltpu.make_async_remote_copy(part(i,blk),part(i,blk),s_sb.at[i,kk],r_main.at[i,kk],device_id=dev((z,y,1-c)),device_id_type=MESH).wait_recv()
+        offload=(C==2 and R%2==0)
+        zx=z+1-2*(z%2)
+        true=c>=0
+        def own(i):
+            b,j=pieces[i]
+            if not j: own_copy(b).wait()
+            send(y>0,i,z,y,(z,y-1,c),s_yd,r_main)
+            send(y<C-1,i,z,y,(z,y+1,c),s_yu,r_main)
+            send(z>0,i,z,y,(z-1,y,c),s_zd,r_main)
+            send(z<R-1,i,z,y,(z+1,y,c),s_zu,r_main)
+            send(true,i,z,y,(z,y,1-c),s_sb,r_sib)
+        def z_arrivals(i):
+            for d in range(1,R):
+                for sign in (-1,1):
+                    zb=z+sign*d
+                    ok=(zb>=0)&(zb<R)
+                    zbc=jnp.clip(zb,0,R-1)
+                    wait_main(ok,i,zbc,y)
+                    if sign<0: send(ok&(z<R-1),i,zbc,y,(z+1,y,c),s_zu,r_main)
+                    else: send(ok&(z>0),i,zbc,y,(z-1,y,c),s_zd,r_main)
+                    ydo=ok&jnp.logical_not((c==1)&(zbc==zx)) if offload else ok
+                    send(ydo&(y>0),i,zbc,y,(z,y-1,c),s_yd,r_main)
+                    send(ydo&(y<C-1),i,zbc,y,(z,y+1,c),s_yu,r_main)
+                    send(ok,i,zbc,y,(z,y,1-c),s_sb,r_sib)
+        def y_arrivals(i,near):
+            for dy in range(1,C):
+                for sign in (-1,1):
+                    yb=y+sign*dy
+                    oky=(yb>=0)&(yb<C)
+                    ybc=jnp.clip(yb,0,C-1)
+                    for d in ([0] if near else range(1,R)):
+                        for zs in ((0,) if d==0 else (-1,1)):
+                            zb=z+zs*d
+                            ok=oky&(zb>=0)&(zb<R)
+                            zbc=jnp.clip(zb,0,R-1)
+                            wait_main(ok,i,zbc,ybc)
+                            if C>2:
+                                if sign<0: send(ok&(y<C-1),i,zbc,ybc,(z,y+1,c),s_yu,r_main)
+                                else: send(ok&(y>0),i,zbc,ybc,(z,y-1,c),s_yd,r_main)
+                            if offload and d==0:
+                                send(ok&(c==1),i,zbc,ybc,(zx,y,c),s_ex,r_main)
+                            send(ok,i,zbc,ybc,(z,y,1-c),s_sb,r_sib)
+        def finish(i):
+            def body(kk,_):
+                blk=kk*2+1-c
+                pltpu.make_async_remote_copy(part(i,blk),part(i,blk),s_sb.at[i,kk],r_sib.at[i,kk],device_id=dev((z,y,1-c)),device_id_type=MESH).wait_recv()
+                return 0
+            lax.fori_loop(0,n//2,body,0)
+        LA=2
+        for i in range(LA): own(i)
+        prepare()
+        for i in range(NP+2):
+            if i+LA<NP: own(i+LA)
+            if i<NP: z_arrivals(i)
+            if 0<=i-1<NP: y_arrivals(i-1,True)
+            if 0<=i-2<NP:
+                y_arrivals(i-2,False)
+                finish(i-2)
+                arrived(i-2)
+    else:
+        prepare()
+        for i in range(NP):
+            b,j=pieces[i]
+            if not j: own_copy(b).wait()
+            arrived(i)
+    @pl.when(sec==1)
+    def _():
+        def forward(m,_):
+            for j in range(D//XC): xcopy(m,j).wait_recv()
+            f_norm(m)
+            f_proj(m,q,Wq); f_proj(m,k,Wk); f_proj(m,v,Wv)
+            f_attend(m,True)
+            f_out(m)
+            f_gate(m)
+            for j in range(D//XC): f_down(m,j)
+            return 0
+        lax.fori_loop(0,micro,forward,0)
+    def gsave(j,i,dst,m): return pltpu.make_async_copy(grads.at[i,pl.ds(pl.multiple_of(m*T,T),T)],dst.at[m],out_sem.at[j,m])
+    def backward(m,_):
+        @pl.when(sec==0)
+        def _(): ecopy(m).wait_recv()
         save(4,so,so_hbm,m).start()
-    def backward(t,m):
-        @pl.when(sec==0)
-        def _(): xcopy(1,m).wait_recv()
         save(5,eg,e_h,m).start()
         def b1(cs):
             hg=nt(eg[m],Wd[cs,:])
@@ -288,18 +422,18 @@
         save(6,g,gi_h,m).start(); save(7,u,ui_h,m).start()
         def b2(cs): acc[:,cs]=nt(g[m],Wg[cs,:])+nt(u[m],Wu[cs,:])
         cols_loop(D,256,b2)
+        ms=pl.ds(pl.multiple_of(m*T,T),T)
         def b3(r):
             t_=eg[m,r,:].astype(jnp.float32)+norm_back(middle[m,r,:],acc[r,:],1)
-            mg[r,:]=t_; grads[0,pl.ds(m*T+r.start,RB),:]=t_.astype(B16)
+            mg[r,:]=t_; grads[0,pl.ds(pl.multiple_of(m*T,T)+r.start,RB),:]=t_.astype(B16)
         rows_loop(b3)
-        ms=pl.ds(pl.multiple_of(m*T,T),T)
-        def gsave(j,i,dst): return pltpu.make_async_copy(grads.at[i,ms],dst.at[m],out_sem.at[j,m])
-        gsave(8,0,ai_h).start()
-        def b4(cs): mxg[:,cs]=nt(grads[0,ms,:],Wo[cs,:]).astype(B16)
+        gsave(8,0,ai_h,m).start()
+        save(0,normed,normed_h,m).wait()
+        def b4(cs): normed[m,:,cs]=nt(grads[0,ms,:],Wo[cs,:]).astype(B16)
         cols_loop(D,256,b4)
         def head(h,_):
             hs=pl.ds(pl.multiple_of(h*HD,HD),HD)
-            qh=q[m,:,hs]; kh=k[m,:,hs]; vh=v[m,:,hs]; mh=mxg[:,hs]
+            qh=q[m,:,hs]; kh=k[m,:,hs]; vh=v[m,:,hs]; mh=normed[m,:,hs]
             ps=p[m,h,:,0:T]; pr=p[m,h,:,T:T+MEMK]
             grads[3,ms,hs]=tn(ps,mh).astype(B16)
             pg=nt(mh,vh)
@@ -311,37 +445,33 @@
             grads[1,ms,hs]=((nn(ds,kh)+qr)*scale).astype(B16)
             grads[2,ms,hs]=(tn(ds,qh)*scale).astype(B16)
             return 0
-        lax.fori_loop(0,HEADS,head,0)
-        gsave(9,1,dq_h).start(); gsave(10,2,dk_h).start(); gsave(11,3,dv_h).start()
+        lax.fori_loop(0,HEADS,head,0,unroll=HEADS)
+        gsave(9,1,dq_h,m).start(); gsave(10,2,dk_h,m).start(); gsave(11,3,dv_h,m).start()
         def b5(cs): acc[:,cs]=nt(grads[1,ms,:],Wq[cs,:])+nt(grads[2,ms,:],Wk[cs,:])+nt(grads[3,ms,:],Wv[cs,:])
         cols_loop(D,256,b5)
         def b6(r): ig[m,r,:]=(mg[r,:]+norm_back(cur[m,r,:].astype(jnp.float32),acc[r,:],0)).astype(B16)
         rows_loop(b6)
         @pl.when(sec==1)
-        def _(): xcopy(1,m).start()
+        def _(): ecopy(m).start()
         save(12,ig,ig_hbm,m).start()
-    def tick(t,_):
-        first=sec==0
-        is_f=jnp.where(first,t<micro,t%2==0)
-        m=jnp.where(first,lax.rem(t,micro),t//2)
-        @pl.when(is_f)
-        def _(): forward(t,m)
-        @pl.when(jnp.logical_not(is_f))
-        def _(): backward(t,m)
         return 0
-    lax.fori_loop(0,2*micro,tick,0)
+    lax.fori_loop(0,micro,backward,0)
+    for cond,mk in pending:
+        @pl.when(cond)
+        def _(mk=mk): mk().wait_send()
     for m in range(micro):
         @pl.when(sec==0)
-        def _(): xcopy(0,m).wait_send()
+        def _():
+            for j in range(D//XC): xcopy(m,j).wait_send()
         @pl.when(sec==1)
-        def _(): xcopy(1,m).wait_send()
-        for j,(s,d) in enumerate([(normed,normed_h),(mixed,mixed_h),(n2,n2_h),(hidden,hidden_h),(so,so_hbm),(eg,e_h),(g,gi_h),(u,ui_h)]):
+        def _(): ecopy(m).wait_send()
+        for j,(s,d) in enumerate([(mixed,mixed_h),(n2,n2_h),(hidden,hidden_h),(so,so_hbm),(eg,e_h),(g,gi_h),(u,ui_h)],1):
             save(j,s,d,m).wait()
         for j,i,d in ((8,0,ai_h),(9,1,dq_h),(10,2,dk_h),(11,3,dv_h)):
-            pltpu.make_async_copy(grads.at[i,pl.ds(m*T,T)],d.at[m],out_sem.at[j,m]).wait()
+            gsave(j,i,d,m).wait()
         save(12,ig,ig_hbm,m).wait()
 
-def chain(n, x, og, docs, mk, mv, midx, mreset, gparts, weights, cid=2):
+def front(n, fused, x, og, docs, mk, mv, midx, mreset, vec, weights, cid=2):
     micro,T,D=x.shape
     FF=weights[4].shape[1]
     CACHE=mk.shape[1]; NBLK=midx.shape[1]
@@ -350,19 +480,22 @@
     act=(micro,T,D); fact=(micro,T,FF)
     S=jax.ShapeDtypeStruct
     outs=[S(act,B),S(act,B),S((8,D),F),S(act,B),S(act,B),S(act,B),S(act,B),S(fact,B),S(fact,B),S(fact,B),S(act,B),S(act,B),S(act,B),S(act,B)]
-    scratch=[V(w.shape,B) for w in weights]
-    scratch+=[V(act,B)]*8+[V(fact,B)]*3+[V(act,F),V((micro,HEADS,T,T+MEMK),B),V((micro,NBLK*MEMK,D),B),V((micro,NBLK*MEMK,D),B),V((4,micro*T,D),B),V((T,D),B),V((T,D),F),V((T,D),F),V(act,B),V(act,B),V((micro,T,T),F),V((8,D),F)]
+    ws=[vec]+list(weights)
+    scratch=[V((n,)+w.shape if fused else w.shape,B) for w in ws]
+    scratch+=[V(act,B)]*8+[V(fact,B)]*3+[V(act,F),V((micro,HEADS,T,T+MEMK),B),V((micro,NBLK*MEMK,D),B),V((micro,NBLK*MEMK,D),B),V((4,micro*T,D),B),V((T,D),F),V((T,D),F),V(act,B),V(act,B),V((micro,T,T),B),V((8,D),F)]
     DM=pltpu.SemaphoreType.DMA
-    scratch+=[DM((7,)),DM((2,)),DM((4,)),DM((13,micro)),DM((2,micro)),DM((2,micro)),DM((1,)),DM((1,))]
+    NP=7+D//XC
+    scratch+=[DM((8,)),DM((2,)),DM((4,)),DM((13,micro)),DM((micro,D//XC)),DM((micro,D//XC)),DM((micro,)),DM((micro,))]
+    scratch+=[DM((NP,n//2) if fused else (1,))]*8
     HB=pl.BlockSpec(memory_space=pltpu.HBM); VB=pl.BlockSpec(memory_space=pltpu.VMEM)
     reset=jnp.broadcast_to(mreset[:,:,None],(micro,NBLK,MEMK))
-    return pl.pallas_call(functools.partial(chain_kernel,n,micro,T,D,FF,CACHE,NBLK),
+    return pl.pallas_call(functools.partial(front_kernel,n,fused,micro,T,D,FF,CACHE,NBLK),
         out_shape=outs,
-        in_specs=[HB,HB,VB,HB,HB,VB,VB,VB]+[HB]*7,
+        in_specs=[HB,HB,VB,HB,HB,VB,VB]+[HB]*8,
         out_specs=[HB,HB,VB]+[HB]*11,
         scratch_shapes=scratch,
         compiler_params=pltpu.CompilerParams(collective_id=cid,has_side_effects=True,vmem_limit_bytes=64<<20),
-    )(x,og,docs,mk,mv,midx,reset,gparts,*weights)
+    )(x,og,docs,mk,mv,midx,reset,*ws)
 
 
 COLS=1024
@@ -650,11 +783,14 @@
     vec = lax.dynamic_update_slice(vec, jnp.concatenate([attend_gain, feed_gain]), (0, f * gw))
     shards = [w[0] for w in (query_weight, key_weight, value_weight, output_weight, gate_weight, up_weight, down_weight)]
     rows = [s.shape[0] for s in shards]
-    padded = [jnp.pad(s, ((0, -s.shape[0] % 16), (0, 0))) for s in shards]
-    gathered = gather(n, [vec] + padded, 0)
-    weights = [g[:, :r].reshape(n * r, g.shape[2]) for g, r in zip(gathered[1:], rows)]
-    (so, ig, gsum, e, normed, mixed, n2, hidden, gi, ui, ai, dq, dk, dv) = chain(
-        n, block_input, output_grad, document_ids, memory_keys, memory_values, memory_index, memory_reset, gathered[0], weights, 2)
+    fused = all(s % 16 == 0 for s in rows)
+    if not fused:
+        padded = [jnp.pad(s, ((0, -s.shape[0] % 16), (0, 0))) for s in shards]
+        gathered = gather(n, [vec] + padded, 0)
+        vec = jnp.sum(gathered[0], axis=0, keepdims=True)
+        shards = [g[:, :r].reshape(n * r, g.shape[2]) for g, r in zip(gathered[1:], rows)]
+    (so, ig, gsum, e, normed, mixed, n2, hidden, gi, ui, ai, dq, dk, dv) = front(
+        n, fused, block_input, output_grad, document_ids, memory_keys, memory_values, memory_index, memory_reset, vec, shards, 2)
     flat = lambda a: a.reshape(micro * T, a.shape[2])
     hid = flat(hidden)
     rd = rows[6]

time: 452 us -> 434 us (0.960); the launches traced: 452 us -> 426 us
  Pallas kernels: 438 us -> 409 us
    pallas_call x2 -> x1, Pallas kernels: 281 us -> 249 us  [front(): pl.pallas_call(functools.partial(front_kernel, n, fused, micro, T, D, FF,...]
    unnamed x25 -> x23, local copies, waits for them, and re-layouts: 10.1 us -> 9.45 us
where the time goes in v2:
time: 434 us; the launch traced here: 426 us
  Pallas kernels  409 us (94%)
  local copies, waits for them, and re-layouts  15.3 us (4%)
    pallas_call x1, Pallas kernels, front(): pl.pallas_call(functools.partial(front_kernel, n, fused, micro, T, D, FF,...  249 us
    pallas_call x1, Pallas kernels, reduce(): pl.pallas_call(functools.partial(reduce_kernel, n, tok, ls, rs, weights,...  160 us
    unnamed x23, local copies, waits for them, and re-layouts  9.45 us

profile of v2, /device:TPU:0, one launch (start us, length us, event | category | flops | bytes accessed | tf_op | source)
XLA Modules:
  0.0 426.2 jit_solution(3032624091539720902)
XLA Ops:
  0.6 0.7 pad_maximum_fusion
  1.3 1.3 broadcast_in_dim.36.refs_6_
  2.7 0.6 broadcast_in_dim.37
  3.3 2.5 dynamic_update_slice.3.refs_7_
  5.8 249.1 %shard_map.239 = (bf16[2,256,1024]{2,1,0:T(8,128)(2,1)}, bf16[2,256,1024]{2,1,0:T(8,128)(2,1)}, f32[8,1024]{1,0:T(8,128)}, bf16[2,256,1024]{2,1,0:T(8,128)(2,1)}...) custom-call(bf16[2,256,1024]{2,1,0:T(8,128)(2,1)} %refs_0_.1, ...), custom_call_target="tpu_custom_call" | custom-call | tf_op jit(solution)/shard_map/pallas_call | solution.py:492
  255.0 160.2 %shard_map.240 = (bf16[176,1024]{1,0:T(8,128)(2,1)}, bf16[64,2816]{1,0:T(8,128)(2,1)}, bf16[64,2816]{1,0:T(8,128)(2,1)}, bf16[64,1024]{1,0:T(8,128)(2,1)}, bf16[...) custom-call(bf16[512,2816]{1,0:T(8,128)(2,1)} %bitcast.27, ...), custom_call_target="tpu_custom_call" | custom-call | tf_op jit(solution)/shard_map/pallas_call | solution.py:762
  415.2 0.0 copy-start.6
  415.2 0.0 copy-start.5
  415.2 0.0 copy-start.4
  415.2 0.0 copy-start.3
  415.2 0.0 copy-start.2
  415.2 0.8 dynamic-slice_convert_fusion
  416.0 0.5 fusion
  416.6 0.0 copy-start.1
  416.6 0.0 copy-start
  416.6 2.3 copy.37
  418.9 2.3 copy.38
  421.2 0.0 copy-done.6
  421.2 0.7 copy.39
  421.8 0.0 copy-done.5
  421.8 0.7 copy.40
  422.5 0.0 copy-done.4
  422.5 0.7 copy.41
  423.1 0.0 copy-done.3
  423.1 0.7 copy.42
  423.8 0.0 copy-done.2
  423.8 0.7 copy.43
  424.5 0.0 copy-done.1
  424.5 0.7 copy.44
  425.3 0.0 copy-done
  425.3 0.7 copy.45
Async XLA Ops:
  415.2 6.0 %copy-start.6 = (bf16[64,1024]{1,0:T(8,128)(2,1)S(1)}, bf16[64,1024]{1,0:T(8,128)(2,1)}, u32[]{:S(2)}) copy-start(bf16[64,1024]{1,0:T(8,128)(2,1)} %get-tuple-element.47) | copy-start | bytes 393220
  415.2 6.7 %copy-start.5 = (bf16[64,1024]{1,0:T(8,128)(2,1)S(1)}, bf16[64,1024]{1,0:T(8,128)(2,1)}, u32[]{:S(2)}) copy-start(bf16[64,1024]{1,0:T(8,128)(2,1)} %get-tuple-element.48) | copy-start | bytes 393220
  415.2 7.3 %copy-start.4 = (bf16[64,1024]{1,0:T(8,128)(2,1)S(1)}, bf16[64,1024]{1,0:T(8,128)(2,1)}, u32[]{:S(2)}) copy-start(bf16[64,1024]{1,0:T(8,128)(2,1)} %get-tuple-element.49) | copy-start | bytes 393220
  415.2 8.0 %copy-start.3 = (bf16[64,1024]{1,0:T(8,128)(2,1)S(1)}, bf16[64,1024]{1,0:T(8,128)(2,1)}, u32[]{:S(2)}) copy-start(bf16[64,1024]{1,0:T(8,128)(2,1)} %get-tuple-element.50) | copy-start | bytes 393220
  415.2 8.6 %copy-start.2 = (bf16[64,2816]{1,0:T(8,128)(2,1)S(1)}, bf16[64,2816]{1,0:T(8,128)(2,1)}, u32[]{:S(2)}) copy-start(bf16[64,2816]{1,0:T(8,128)(2,1)} %get-tuple-element.51) | copy-start | bytes 1081348
  416.6 8.0 %copy-start.1 = (bf16[64,2816]{1,0:T(8,128)(2,1)S(1)}, bf16[64,2816]{1,0:T(8,128)(2,1)}, u32[]{:S(2)}) copy-start(bf16[64,2816]{1,0:T(8,128)(2,1)} %get-tuple-element.52) | copy-start | bytes 1081348
  416.6 8.7 %copy-start = (bf16[176,1024]{1,0:T(8,128)(2,1)S(1)}, bf16[176,1024]{1,0:T(8,128)(2,1)}, u32[]{:S(2)}) copy-start(bf16[176,1024]{1,0:T(8,128)(2,1)} %get-tuple-element.53) | copy-start | bytes 1081348

commit v3 on v2

--- a/solution.py
+++ b/solution.py
@@ -133,7 +133,7 @@
 def front_kernel(n, fused, micro, T, D, FF, CACHE, NBLK, *refs):
     it=iter(refs)
     take=lambda k:[next(it) for _ in range(k)]
-    x_hbm,og_hbm,docs,mk_hbm,mv_hbm,midx,mreset=take(7)
+    x_hbm,og_hbm,docs,mk_hbm,mv_hbm,midx,mreset,again,fgain=take(9)
     ins=take(8)
     (so_hbm,ig_hbm,gsum,e_h,normed_h,mixed_h,n2_h,hidden_h,gi_h,ui_h,ai_h,dq_h,dk_h,dv_h)=take(14)
     bufs=take(8)
@@ -159,7 +159,11 @@
         def _(d=d): pl.semaphore_signal(bar,1,device_id=d,device_id_type=MESH)
     def own_copy(i):
         return pltpu.make_async_copy(ins[i],bufs[i].at[f] if fused else bufs[i],own_sem.at[i])
-    for i in range(8): own_copy(i).start()
+    for i in range(8):
+        if i or not fused: own_copy(i).start()
+    if fused:
+        both=jnp.concatenate([again[...].astype(jnp.float32),fgain[...].astype(jnp.float32)],axis=1)
+        bufs[0][f]=jnp.broadcast_to(both,bufs[0].shape[1:]).astype(B16)
     def load_cur(): return pltpu.make_async_copy(x_hbm,cur,in_sem.at[0])
     def load_eg(): return pltpu.make_async_copy(og_hbm,eg,in_sem.at[0])
     HC=CACHE//2
@@ -204,31 +208,38 @@
     def f_proj(m,dst,w):
         def f2(cs): dst[m,:,cs]=nn(normed[m],w[:,cs]).astype(B16)
         cols_loop(D,256,f2)
+    G=4
+    def by_block(a,other,hs,m,fn):
+        return jnp.concatenate([fn(a[b*MQB:(b+1)*MQB],other[m,b*MEMK:(b+1)*MEMK,hs]) for b in range(NBLK)],axis=0)
+    def halves(a): return [a[:,i:i+HD] for i in range(0,T,HD)]
+    def row_sum(*parts): return jnp.sum(functools.reduce(jnp.add,parts),axis=-1,keepdims=True)
+    def row_max(*parts): return jnp.max(functools.reduce(jnp.maximum,parts),axis=-1,keepdims=True)
     def f_attend(m,recall):
-        def head(h,_):
-            hs=pl.ds(pl.multiple_of(h*HD,HD),HD)
-            qh=q[m,:,hs]; kh=k[m,:,hs]; vh=v[m,:,hs]
-            s=jnp.where(mask[m].astype(jnp.float32)>0.5,nt(qh,kh)*scale,MASKED)
-            if not recall:
-                es_=jnp.exp(s-jnp.max(s,axis=-1,keepdims=True))
-                ps=(es_*(1.0/jnp.sum(es_,axis=-1,keepdims=True))).astype(B16)
-                p[m,h,:,0:T]=ps
-                mixed[m,:,hs]=nn(ps,vh).astype(B16)
-                return 0
-            sr=[]
-            for b in range(NBLK):
-                x=nt(qh[b*MQB:(b+1)*MQB],rk[m,b*MEMK:(b+1)*MEMK,hs])*scale
-                sr.append(jnp.where(jnp.broadcast_to(mreset[m,b:b+1,:]==0,(MQB,MEMK)),x,MASKED))
-            sr=jnp.concatenate(sr,axis=0)
-            top=jnp.maximum(jnp.max(s,axis=-1,keepdims=True),jnp.max(sr,axis=-1,keepdims=True))
-            es_=jnp.exp(s-top); er_=jnp.exp(sr-top)
-            inv=1.0/(jnp.sum(es_,axis=-1,keepdims=True)+jnp.sum(er_,axis=-1,keepdims=True))
-            ps=(es_*inv).astype(B16); pr=(er_*inv).astype(B16)
-            p[m,h,:,0:T]=ps; p[m,h,:,T:T+MEMK]=pr
-            mr=jnp.concatenate([nn(pr[b*MQB:(b+1)*MQB],rv[m,b*MEMK:(b+1)*MEMK,hs]) for b in range(NBLK)],axis=0)
-            mixed[m,:,hs]=(nn(ps,vh)+mr).astype(B16)
-            return 0
-        lax.fori_loop(0,HEADS,head,0,unroll=HEADS)
+        for h0 in range(0,HEADS,G):
+            HS=[slice(h*HD,h*HD+HD) for h in range(h0,h0+G)]
+            qs=[q[m,:,hs] for hs in HS]
+            s=[nt(a,k[m,:,hs]) for a,hs in zip(qs,HS)]
+            if recall: x=[by_block(a,rk,hs,m,nt) for a,hs in zip(qs,HS)]
+            ok=mask[m].astype(jnp.float32)>0.5
+            s=[jnp.where(ok,a*scale,MASKED) for a in s]
+            if recall:
+                live=jnp.concatenate([jnp.broadcast_to(mreset[pl.ds(m,1),b:b+1],(MQB,MEMK)) for b in range(NBLK)],axis=0)==0
+                x=[jnp.where(live,a*scale,MASKED) for a in x]
+                top=[row_max(b,*halves(a)) for a,b in zip(s,x)]
+                xe=[jnp.exp(b-t) for b,t in zip(x,top)]
+            else: top=[row_max(*halves(a)) for a in s]
+            se=[jnp.exp(a-t) for a,t in zip(s,top)]
+            if recall: inv=[1.0/row_sum(b,*halves(a)) for a,b in zip(se,xe)]
+            else: inv=[1.0/row_sum(*halves(a)) for a in se]
+            ps=[(a*i).astype(B16) for a,i in zip(se,inv)]
+            o=[nn(a,v[m,:,hs]) for a,hs in zip(ps,HS)]
+            if recall:
+                pr=[(a*i).astype(B16) for a,i in zip(xe,inv)]
+                o=[a+by_block(b,rv,hs,m,nn) for a,b,hs in zip(o,pr,HS)]
+            for j in range(G):
+                p[m,h0+j,:,0:T]=ps[j]
+                if recall: p[m,h0+j,:,T:T+MEMK]=pr[j]
+                mixed[m,:,HS[j]]=o[j].astype(B16)
         save(1,mixed,mixed_h,m).start()
     def f_out(m):
         def f3(cs): middle[m,:,cs]=cur[m,:,cs].astype(jnp.float32)+nn(mixed[m],Wo[:,cs])
@@ -240,8 +251,10 @@
         def f5(cs):
             a=n2[m]
             gg=nn(a,Wg[:,cs]); uu=nn(a,Wu[:,cs])
-            g[m,:,cs]=gg.astype(B16); u[m,:,cs]=uu.astype(B16)
-            hidden[m,:,cs]=(gg*jax.nn.sigmoid(gg)*uu).astype(B16)
+            sg=jax.nn.sigmoid(gg)
+            act=gg*sg
+            g[m,:,cs]=(uu*(sg*(1.0+gg*(1.0-sg)))).astype(B16); u[m,:,cs]=act.astype(B16)
+            hidden[m,:,cs]=(act*uu).astype(B16)
         cols_loop(FF,256,f5)
         save(3,hidden,hidden_h,m).start()
     def f_down(m,j):
@@ -262,8 +275,16 @@
         if m+1<micro:
             for cp in load_cache(m+1,kv): cp.start()
     def setup():
-        parts=bufs[0][...]
-        gain[...]=jnp.sum(parts.astype(jnp.float32),axis=0)[0:8]
+        if not fused:
+            gain[...]=bufs[0][0,0:8,:].astype(jnp.float32)
+            return
+        lane=lax.broadcasted_iota(jnp.int32,(8,128),1)
+        for e in range(n//2):
+            lo=bufs[0][2*e].astype(jnp.float32)[0:8]
+            hi=bufs[0][2*e+1].astype(jnp.float32)[0:8]
+            cs=pl.ds(e*128,128)
+            gain[0:1,cs]=jnp.where(lane<64,lo,pltpu.roll(hi,64,1))[0:1]
+            gain[1:2,cs]=jnp.where(lane<64,pltpu.roll(lo,64,1),hi)[0:1]
     def each(fn):
         def b(m,_):
             fn(m); return 0
@@ -296,18 +317,7 @@
             row=jnp.broadcast_to(docs[m:m+1,:].astype(jnp.float32),(T,T))
             mask[m]=jnp.where((row==row.T)&(ci<=ri),1.0,0.0).astype(B16)
         @pl.when(sec==0)
-        def _():
-            def zero(i,_):
-                o=pl.ds(pl.multiple_of(i*MEMK,MEMK),MEMK)
-                for m in range(micro):
-                    rk[m,o,:]=jnp.zeros((MEMK,D),B16); rv[m,o,:]=jnp.zeros((MEMK,D),B16)
-                return 0
-            lax.fori_loop(0,NBLK,zero,0)
-            def zero_p(h,_):
-                for m in range(micro): p[m,h,:,T:T+MEMK]=jnp.zeros((T,MEMK),B16)
-                return 0
-            lax.fori_loop(0,HEADS,zero_p,0)
-            load_cur().wait()
+        def _(): load_cur().wait()
         @pl.when(sec==1)
         def _(): load_eg().wait()
     pl.semaphore_wait(bar,sum(jnp.where(cond,1,0) for cond,d in nb))
@@ -334,14 +344,14 @@
         true=c>=0
         def own(i):
             b,j=pieces[i]
-            if not j: own_copy(b).wait()
+            if not j and b: own_copy(b).wait()
             send(y>0,i,z,y,(z,y-1,c),s_yd,r_main)
             send(y<C-1,i,z,y,(z,y+1,c),s_yu,r_main)
             send(z>0,i,z,y,(z-1,y,c),s_zd,r_main)
             send(z<R-1,i,z,y,(z+1,y,c),s_zu,r_main)
             send(true,i,z,y,(z,y,1-c),s_sb,r_sib)
-        def z_arrivals(i):
-            for d in range(1,R):
+        def z_arrivals(i,d):
+            if True:
                 for sign in (-1,1):
                     zb=z+sign*d
                     ok=(zb>=0)&(zb<R)
@@ -378,22 +388,27 @@
                 return 0
             lax.fori_loop(0,n//2,body,0)
         LA=2
+        LAST=R
         for i in range(LA): own(i)
         prepare()
-        for i in range(NP+2):
+        for i in range(NP+LAST):
             if i+LA<NP: own(i+LA)
-            if i<NP: z_arrivals(i)
+            for d in range(1,R):
+                if 0<=i-d+1<NP: z_arrivals(i-d+1,d)
             if 0<=i-1<NP: y_arrivals(i-1,True)
-            if 0<=i-2<NP:
-                y_arrivals(i-2,False)
-                finish(i-2)
-                arrived(i-2)
+            if 0<=i-LAST+1<NP:
+                y_arrivals(i-LAST+1,False)
+                finish(i-LAST+1)
+                arrived(i-LAST+1)
     else:
         prepare()
         for i in range(NP):
             b,j=pieces[i]
             if not j: own_copy(b).wait()
             arrived(i)
+    for cond,mk in pending:
+        @pl.when(cond)
+        def _(mk=mk): mk().wait_send()
     @pl.when(sec==1)
     def _():
         def forward(m,_):
@@ -407,6 +422,29 @@
             return 0
         lax.fori_loop(0,micro,forward,0)
     def gsave(j,i,dst,m): return pltpu.make_async_copy(grads.at[i,pl.ds(pl.multiple_of(m*T,T),T)],dst.at[m],out_sem.at[j,m])
+    def b_attend(m,ms,recall):
+        for h0 in range(0,HEADS,G):
+            HS=[slice(h*HD,h*HD+HD) for h in range(h0,h0+G)]
+            mh=[normed[m,:,hs] for hs in HS]
+            ps=[p[m,h,:,0:T] for h in range(h0,h0+G)]
+            pg=[nt(a,v[m,:,hs]) for a,hs in zip(mh,HS)]
+            if recall:
+                pr=[p[m,h,:,T:T+MEMK].astype(jnp.float32) for h in range(h0,h0+G)]
+                rg=[by_block(a,rv,hs,m,nt) for a,hs in zip(mh,HS)]
+            dv=[tn(a,b) for a,b in zip(ps,mh)]
+            pf=[a.astype(jnp.float32) for a in ps]
+            if recall:
+                w=[row_sum(c_*d_,*halves(a*b)) for a,b,c_,d_ in zip(pf,pg,pr,rg)]
+                dr=[(a*(b-t)).astype(B16) for a,b,t in zip(pr,rg,w)]
+            else: w=[row_sum(*halves(a*b)) for a,b in zip(pf,pg)]
+            ds=[(a*(b-t)).astype(B16) for a,b,t in zip(pf,pg,w)]
+            dq=[nn(a,k[m,:,hs]) for a,hs in zip(ds,HS)]
+            if recall: dq=[a+by_block(b,rk,hs,m,nn) for a,b,hs in zip(dq,dr,HS)]
+            dk=[tn(a,q[m,:,hs]) for a,hs in zip(ds,HS)]
+            for j in range(G):
+                grads[3,ms,HS[j]]=dv[j].astype(B16)
+                grads[1,ms,HS[j]]=(dq[j]*scale).astype(B16)
+                grads[2,ms,HS[j]]=(dk[j]*scale).astype(B16)
     def backward(m,_):
         @pl.when(sec==0)
         def _(): ecopy(m).wait_recv()
@@ -414,10 +452,8 @@
         save(5,eg,e_h,m).start()
         def b1(cs):
             hg=nt(eg[m],Wd[cs,:])
-            gg=g[m,:,cs].astype(jnp.float32); uu=u[m,:,cs].astype(jnp.float32)
-            sg=jax.nn.sigmoid(gg)
-            u[m,:,cs]=(hg*gg*sg).astype(B16)
-            g[m,:,cs]=(hg*uu*sg*(1.0+gg*(1.0-sg))).astype(B16)
+            u[m,:,cs]=(hg*u[m,:,cs].astype(jnp.float32)).astype(B16)
+            g[m,:,cs]=(hg*g[m,:,cs].astype(jnp.float32)).astype(B16)
         cols_loop(FF,256,b1)
         save(6,g,gi_h,m).start(); save(7,u,ui_h,m).start()
         def b2(cs): acc[:,cs]=nt(g[m],Wg[cs,:])+nt(u[m],Wu[cs,:])
@@ -431,21 +467,8 @@
         save(0,normed,normed_h,m).wait()
         def b4(cs): normed[m,:,cs]=nt(grads[0,ms,:],Wo[cs,:]).astype(B16)
         cols_loop(D,256,b4)
-        def head(h,_):
-            hs=pl.ds(pl.multiple_of(h*HD,HD),HD)
-            qh=q[m,:,hs]; kh=k[m,:,hs]; vh=v[m,:,hs]; mh=normed[m,:,hs]
-            ps=p[m,h,:,0:T]; pr=p[m,h,:,T:T+MEMK]
-            grads[3,ms,hs]=tn(ps,mh).astype(B16)
-            pg=nt(mh,vh)
-            rg=jnp.concatenate([nt(mh[b*MQB:(b+1)*MQB],rv[m,b*MEMK:(b+1)*MEMK,hs]) for b in range(NBLK)],axis=0)
-            pf=ps.astype(jnp.float32); rf=pr.astype(jnp.float32)
-            w=jnp.sum(pf*pg,axis=-1,keepdims=True)+jnp.sum(rf*rg,axis=-1,keepdims=True)
-            ds=(pf*(pg-w)).astype(B16); dr=(rf*(rg-w)).astype(B16)
-            qr=jnp.concatenate([nn(dr[b*MQB:(b+1)*MQB],rk[m,b*MEMK:(b+1)*MEMK,hs]) for b in range(NBLK)],axis=0)
-            grads[1,ms,hs]=((nn(ds,kh)+qr)*scale).astype(B16)
-            grads[2,ms,hs]=(tn(ds,qh)*scale).astype(B16)
-            return 0
-        lax.fori_loop(0,HEADS,head,0,unroll=HEADS)
+        pl.when(sec==0)(lambda: b_attend(m,ms,False))
+        pl.when(sec==1)(lambda: b_attend(m,ms,True))
         gsave(9,1,dq_h,m).start(); gsave(10,2,dk_h,m).start(); gsave(11,3,dv_h,m).start()
         def b5(cs): acc[:,cs]=nt(grads[1,ms,:],Wq[cs,:])+nt(grads[2,ms,:],Wk[cs,:])+nt(grads[3,ms,:],Wv[cs,:])
         cols_loop(D,256,b5)
@@ -456,9 +479,6 @@
         save(12,ig,ig_hbm,m).start()
         return 0
     lax.fori_loop(0,micro,backward,0)
-    for cond,mk in pending:
-        @pl.when(cond)
-        def _(mk=mk): mk().wait_send()
     for m in range(micro):
         @pl.when(sec==0)
         def _():
@@ -471,7 +491,7 @@
             gsave(j,i,d,m).wait()
         save(12,ig,ig_hbm,m).wait()
 
-def front(n, fused, x, og, docs, mk, mv, midx, mreset, vec, weights, cid=2):
+def front(n, fused, x, og, docs, mk, mv, midx, mreset, again, fgain, vec, weights, cid=2):
     micro,T,D=x.shape
     FF=weights[4].shape[1]
     CACHE=mk.shape[1]; NBLK=midx.shape[1]
@@ -481,31 +501,35 @@
     S=jax.ShapeDtypeStruct
     outs=[S(act,B),S(act,B),S((8,D),F),S(act,B),S(act,B),S(act,B),S(act,B),S(fact,B),S(fact,B),S(fact,B),S(act,B),S(act,B),S(act,B),S(act,B)]
     ws=[vec]+list(weights)
-    scratch=[V((n,)+w.shape if fused else w.shape,B) for w in ws]
+    scratch=[V((n,16,128),B) if fused else V(vec.shape,B)]
+    scratch+=[V((n,)+w.shape if fused else w.shape,B) for w in weights]
     scratch+=[V(act,B)]*8+[V(fact,B)]*3+[V(act,F),V((micro,HEADS,T,T+MEMK),B),V((micro,NBLK*MEMK,D),B),V((micro,NBLK*MEMK,D),B),V((4,micro*T,D),B),V((T,D),F),V((T,D),F),V(act,B),V(act,B),V((micro,T,T),B),V((8,D),F)]
     DM=pltpu.SemaphoreType.DMA
     NP=7+D//XC
     scratch+=[DM((8,)),DM((2,)),DM((4,)),DM((13,micro)),DM((micro,D//XC)),DM((micro,D//XC)),DM((micro,)),DM((micro,))]
     scratch+=[DM((NP,n//2) if fused else (1,))]*8
     HB=pl.BlockSpec(memory_space=pltpu.HBM); VB=pl.BlockSpec(memory_space=pltpu.VMEM)
-    reset=jnp.broadcast_to(mreset[:,:,None],(micro,NBLK,MEMK))
     return pl.pallas_call(functools.partial(front_kernel,n,fused,micro,T,D,FF,CACHE,NBLK),
         out_shape=outs,
-        in_specs=[HB,HB,VB,HB,HB,VB,VB]+[HB]*8,
+        in_specs=[HB,HB,VB,HB,HB,VB,VB,VB,VB]+[HB]*8,
         out_specs=[HB,HB,VB]+[HB]*11,
         scratch_shapes=scratch,
         compiler_params=pltpu.CompilerParams(collective_id=cid,has_side_effects=True,vmem_limit_bytes=64<<20),
-    )(x,og,docs,mk,mv,midx,reset,*ws)
+    )(x,og,docs,mk,mv,midx,mreset,again,fgain,*ws)
 
 
 COLS=1024
-def plan(n, lhs_shapes, rhs_shapes, weights):
+NOFF=99
+def plan(n, lhs_shapes, rhs_shapes, weights, steps):
     pieces=[]
     for w,(l,r) in enumerate(weights):
         rows=lhs_shapes[l][1]//n; N=rhs_shapes[r][1]
-        step=512 if rows>64*16//n else 1024
-        for c0 in range(0,N,step):
-            pieces.append((w,rows,c0,min(step,N-c0)))
+        c0=0
+        for step in steps[w]:
+            pieces.append((w,rows,c0,step)); c0+=step
+        while c0<N:
+            step=min(steps[w][-1],N-c0)
+            pieces.append((w,rows,c0,step)); c0+=step
     return pieces
 
 def reduce_kernel(n, tok, lhs_shapes, rhs_shapes, weights, pieces, vec_rows, SLOTS, *refs):
@@ -517,13 +541,13 @@
     outs=take(NW); vec_out=next(it)
     ring=next(it); tbuf=take(NL)
     keep=take(NP); sibr=take(NP); yr=take(NP); xr=take(NP); zu=take(NP); zd=take(NP); fin=take(NP)
-    shapes=sorted({(p[1],p[3]) for p in pieces})
+    shapes=sorted({p[1] for p in pieces})
     stage_of=dict(zip(shapes,take(len(shapes))))
     vecb=next(it); vecr=next(it)
     (ld_sem,sib_s,sib_r,y_s,y_r,x_s,x_r,zu_s,zu_r,zd_s,zd_r,v_s,v_r,o_s)=take(14)
     sec=lax.axis_index("section"); f=lax.axis_index("fsdp")
     c=f%2; zy=f//2; y=zy%C; z=zy//C
-    offload=(C==2 and R%2==0)
+    OFF=lambda i: C==2 and R%2==0 and i<NOFF
     zx=z+1-2*(z%2)
     def dev(zz,yy,cc): return (sec,(zz*C+yy)*2+cc)
     def rcopy(src,dst,ss,rs,d):
@@ -584,7 +608,8 @@
     for i,(w,rows,c0,nc) in enumerate(pieces):
         l,r=weights[w]
         last_use[load_id[("r",r)][c0//COLS]]=i
-    sends=[]
+    sends={}
+    cur_piece=[0]
     stage_use={}
     def compute(i):
         w,rows,c0,nc=pieces[i]
@@ -593,13 +618,12 @@
         k=load_id[("r",r)][c0//COLS]
         wait_load(k)
         lc=c0%COLS
-        st=stage_of[(rows,nc)]
-        u=stage_use.get((rows,nc),0); stage_use[(rows,nc)]=u+1
-        slot=u%2
-        if u>=2: sib_waits[(rows,nc)].pop(0)()
+        u=stage_use.get(rows,0); stage_use[rows]=u+1
+        st=stage_of[rows].at[u%2,:,:,pl.ds(0,nc)]
+        if u>=2: sib_waits[rows].pop(0)()
         T4=tbuf[l].reshape(H,2,rows,tok)
         CH=256
-        for which,dst in ((1-c,st.at[slot]),(c,keep[i])):
+        for which,dst in ((1-c,st),(c,keep[i])):
             def body(j,_,which=which,dst=dst):
                 o=pl.multiple_of(j*CH,CH)
                 a=T4[:,which].reshape(H*rows,tok)
@@ -609,9 +633,9 @@
                 return 0
             lax.fori_loop(0,nc//CH,body,0)
             if dst is not keep[i]:
-                cp=rcopy(st.at[slot],sibr[i],sib_s.at[i],sib_r.at[i],(z,y,1-c))
+                cp=rcopy(st,sibr[i],sib_s.at[i],sib_r.at[i],(z,y,1-c))
                 cp.start()
-                sib_waits.setdefault((rows,nc),[]).append(cp.wait_send)
+                sib_waits.setdefault(rows,[]).append(cp.wait_send)
         if last_use[k]==i:
             freed.add(k); pump()
     sib_waits={}
@@ -621,12 +645,12 @@
             dst[pl.ds(o,16),:]=dst[pl.ds(o,16),:]+src[pl.ds(o,16),:]
             return 0
         lax.fori_loop(0,rows//16,body,0)
-    def send(cond,cp):
+    def send(tag,cond,cp):
         if cond is None: cp().start()
         else:
             @pl.when(cond)
             def _(): cp().start()
-        sends.append((cond,cp))
+        sends.setdefault(tag,[]).append((cond,cp))
     def sib_add(i):
         w,rows,c0,nc=pieces[i]
         rcopy(sibr[i],sibr[i],sib_s.at[i],sib_r.at[i],(z,y,1-c)).wait_recv()
@@ -634,8 +658,9 @@
             add_into(keep[i].at[k],sibr[i].at[k],rows)
             return 0
         lax.fori_loop(0,H,body,0)
+        offload=OFF(i)
         if offload:
-            send(c==1,lambda: rcopy(keep[i].at[zx*C+1-y],xr[i],x_s.at[i],x_r.at[i],(zx,y,c)))
+            send((i,'y'),c==1,lambda: rcopy(keep[i].at[zx*C+1-y],xr[i],x_s.at[i],x_r.at[i],(zx,y,c)))
         for kz in range(R-1,-1,-1):
             zt=lax.rem(z+kz,R)
             for ky in range(1,C):
@@ -644,17 +669,18 @@
                 cp=lambda zt=zt,yt=yt,slot=slot: rcopy(keep[i].at[zt*C+yt],yr[i].at[slot,zt],y_s.at[i,slot,zt],y_r.at[i,slot,zt],(z,yt,c))
                 if offload and kz==0:
                     continue
-                send((jnp.logical_not((c==1)&(zt==zx))) if offload else None,cp)
+                send((i,'y'),(jnp.logical_not((c==1)&(zt==zx))) if offload else None,cp)
     def x_add(i):
         w,rows,c0,nc=pieces[i]
-        if not offload: return
+        if not OFF(i): return
         @pl.when(c==1)
         def _():
             rcopy(xr[i],xr[i],x_s.at[i],x_r.at[i],(zx,y,c)).wait_recv()
             add_into(keep[i].at[z*C+1-y],xr[i],rows)
-        send(None,lambda: rcopy(keep[i].at[z*C+1-y],yr[i].at[0,z],y_s.at[i,0,z],y_r.at[i,0,z],(z,1-y,c)))
+        send((i,'y'),None,lambda: rcopy(keep[i].at[z*C+1-y],yr[i].at[0,z],y_s.at[i,0,z],y_r.at[i,0,z],(z,1-y,c)))
     def y_add(i):
         w,rows,c0,nc=pieces[i]
+        offload=OFF(i)
         for kz in range(R-1,-1,-1):
             zt=lax.rem(z+kz,R)
             for slot in range(C-1):
@@ -682,7 +708,7 @@
                         add_into(keep[i].at[t*C+y],rb[i].at[k],rows)
                     cp().start()
             pl.when(z==zs)(go)
-            for k,cp,t in cps: sends.append((z==zs,cp))
+            for k,cp,t in cps: sends.setdefault((i,zs if up else R-1-zs),[]).append((z==zs,cp))
         line(s,True)
         line(R-1-s,False)
     def final(i):
@@ -713,6 +739,12 @@
         return pltpu.make_async_remote_copy(vecb.at[k],vecr.at[k],v_s.at[k],v_r.at[k],device_id=(sec,f^(1<<k)),device_id_type=MESH)
     cp=pltpu.make_async_copy(vec,vecb.at[0],o_s.at[NP]); cp.start(); cp.wait()
     pl.semaphore_wait(bar,sum(jnp.where(cond,1,0) for cond,d in nb))
+    def end_sends(tag):
+        for cond,cp in sends.pop(tag,[]):
+            if cond is None: cp().wait_send()
+            else:
+                @pl.when(cond)
+                def _(cp=cp): cp().wait_send()
     LAGY=3
     for t in range(NP+LAGY+R+1):
         if t<NP: compute(t)
@@ -725,29 +757,27 @@
             if 0<=i<NP: z_step(i,s)
         i=t-LAGY-R
         if 0<=i<NP: final(i)
+        end_sends((t-LAGY-1,'y'))
+        for s in range(R): end_sends((t-LAGY-s-2,s))
     for q in sib_waits.values():
         for wfn in q: wfn()
-    for cond,cp in sends:
-        if cond is None: cp().wait_send()
-        else:
-            @pl.when(cond)
-            def _(): cp().wait_send()
+    for tag in list(sends): end_sends(tag)
     for i in range(NP):
         w,rows,c0,nc=pieces[i]
         pltpu.make_async_copy(fin[i],outs[w].at[:,pl.ds(c0,nc)],o_s.at[i]).wait()
     pltpu.make_async_copy(vecb.at[LOGN],vec_out,o_s.at[NP]).wait()
 
-def reduce(n, lhs, rhs, weights, vec, cid=1, SLOTS=6):
+def reduce(n, lhs, rhs, weights, vec, steps, cid=1, SLOTS=6):
     tok=lhs[0].shape[0]
     ls=[a.shape for a in lhs]; rs=[a.shape for a in rhs]
-    pieces=plan(n,ls,rs,weights)
+    pieces=plan(n,ls,rs,weights,steps)
     R,C=layout(n); H=n//2
     NP=len(pieces)
     LOGN=n.bit_length()-1
     D=pltpu.SemaphoreType.DMA
     B=jnp.bfloat16
     V=pltpu.VMEM
-    shapes=sorted({(p[1],p[3]) for p in pieces})
+    shapes=sorted({(p[1],max(o[3] for o in pieces if o[1]==p[1])) for p in pieces})
     scratch=[V((SLOTS,tok,COLS),B)]+[V((s[1],tok),B) for s in ls]
     scratch+=[V((H,p[1],p[3]),B) for p in pieces]
     scratch+=[V((H,p[1],p[3]),B) for p in pieces]
@@ -769,6 +799,45 @@
     return res[:-1],res[-1]
 
 
+def settle_kernel(count, gw, *refs):
+    ins = refs[:count]
+    total = refs[count]
+    outs = refs[count + 1 : 2 * count + 1]
+    again, fgain = refs[2 * count + 1 : 2 * count + 3]
+    held = refs[2 * count + 3 : 3 * count + 3]
+    in_sem, out_sem = refs[3 * count + 3 :]
+    load = [pltpu.make_async_copy(a, h, in_sem.at[i]) for i, (a, h) in enumerate(zip(ins, held))]
+    store = [pltpu.make_async_copy(h, b.at[0], out_sem.at[i]) for i, (h, b) in enumerate(zip(held, outs))]
+    for cp in load:
+        cp.start()
+    width = total.shape[1]
+    f = lax.axis_index("fsdp")
+    mine = pltpu.roll(total[...], lax.rem(width - f * gw, width), 1)
+    again[...] = mine[0:1, 0:gw].astype(again.dtype)
+    fgain[...] = mine[1:2, 0:gw].astype(fgain.dtype)
+    for cp, out in zip(load, store):
+        cp.wait()
+        out.start()
+    for cp in store:
+        cp.wait()
+
+
+def settle(*arrays):
+    *ins, total = arrays
+    gw = total.shape[1] // lax.axis_size("fsdp")
+    HB = pl.BlockSpec(memory_space=pltpu.HBM)
+    VB = pl.BlockSpec(memory_space=pltpu.VMEM)
+    S = jax.ShapeDtypeStruct
+    return pl.pallas_call(
+        functools.partial(settle_kernel, len(ins), gw),
+        out_shape=[S((1,) + a.shape, a.dtype) for a in ins] + [S((1, gw), jnp.bfloat16)] * 2,
+        in_specs=[HB] * len(ins) + [VB],
+        out_specs=[HB] * len(ins) + [VB] * 2,
+        scratch_shapes=[pltpu.VMEM(a.shape, a.dtype) for a in ins] + [pltpu.SemaphoreType.DMA((len(ins),))] * 2,
+        compiler_params=pltpu.CompilerParams(vmem_limit_bytes=63 << 20),
+    )(*ins, total)
+
+
 def per_device(
     block_input, output_grad, document_ids, memory_keys, memory_values, memory_index, memory_reset,
     query_weight, key_weight, value_weight, output_weight, gate_weight, up_weight, down_weight,
@@ -779,18 +848,19 @@
     micro, T, D = block_input.shape
     FF = gate_weight.shape[2]
     gw = attend_gain.shape[1]
-    vec = jnp.zeros((16, D), jnp.bfloat16)
-    vec = lax.dynamic_update_slice(vec, jnp.concatenate([attend_gain, feed_gain]), (0, f * gw))
     shards = [w[0] for w in (query_weight, key_weight, value_weight, output_weight, gate_weight, up_weight, down_weight)]
     rows = [s.shape[0] for s in shards]
-    fused = all(s % 16 == 0 for s in rows)
+    fused = 2 * gw == 128 and all(s % 16 == 0 for s in rows)
+    vec = attend_gain
     if not fused:
+        vec = jnp.zeros((16, D), jnp.bfloat16)
+        vec = lax.dynamic_update_slice(vec, jnp.concatenate([attend_gain, feed_gain]), (0, f * gw))
         padded = [jnp.pad(s, ((0, -s.shape[0] % 16), (0, 0))) for s in shards]
         gathered = gather(n, [vec] + padded, 0)
         vec = jnp.sum(gathered[0], axis=0, keepdims=True)
         shards = [g[:, :r].reshape(n * r, g.shape[2]) for g, r in zip(gathered[1:], rows)]
     (so, ig, gsum, e, normed, mixed, n2, hidden, gi, ui, ai, dq, dk, dv) = front(
-        n, fused, block_input, output_grad, document_ids, memory_keys, memory_values, memory_index, memory_reset, vec, shards, 2)
+        n, fused, block_input, output_grad, document_ids, memory_keys, memory_values, memory_index, memory_reset, attend_gain, feed_gain, vec, shards, 2)
     flat = lambda a: a.reshape(micro * T, a.shape[2])
     hid = flat(hidden)
     rd = rows[6]
@@ -798,11 +868,11 @@
         hid = jnp.pad(hid.reshape(micro * T, n, rd), ((0, 0), (0, 0), (0, -rd % 16))).reshape(micro * T, -1)
     lhs = [hid, flat(n2), flat(mixed), flat(normed)]
     rhs = [flat(a) for a in (e, gi, ui, ai, dv, dk, dq)]
-    order = [(0, 0), (1, 1), (1, 2), (2, 3), (3, 4), (3, 5), (3, 6)]
-    sums, total = reduce(n, lhs, rhs, order, gsum, 1)
-    gd, gg, gu, go, gv, gk, gq = sums
-    gains = lax.dynamic_slice(total, (0, f * gw), (2, gw)).astype(jnp.bfloat16)
-    return (so[None], ig[None], gq[None], gk[None], gv[None], go[None], gg[None], gu[None], gd[:rd][None], gains[0:1], gains[1:2])
+    order = [(1, 1), (1, 2), (0, 0), (2, 3), (3, 4), (3, 5), (3, 6)]
+    steps = [(512, 512, 1024), (1024,), (512,), (1024,), (1024,), (1024,), (512,)]
+    sums, total = reduce(n, lhs, rhs, order, gsum, steps, 1)
+    gg, gu, gd, go, gv, gk, gq = sums
+    return settle(so, ig, gq, gk, gv, go, gg, gu, gd[:rd], total)
 
 
 def solution(mesh):

time: 434 us -> 390 us (0.90)
  Pallas kernels: 409 us -> 382 us
  local copies, waits for them, and re-layouts: 15.3 us -> 0 us
    pallas_call x1, Pallas kernels: 249 us -> 223 us  [front(): pl.pallas_call(functools.partial(front_kernel, n, fused, micro, T, D, FF,...]
    unnamed x23 -> x0, local copies, waits for them, and re-layouts: 9.45 us -> none
    pallas_call x1, Pallas kernels: 160 us -> 155 us  [reduce(): pl.pallas_call(functools.partial(reduce_kernel, n, tok, ls, rs, weights,...]
    pallas_call x0 -> x1, Pallas kernels: none -> 4.5 us  [settle(): pl.pallas_call(functools.partial(settle_kernel, len(ins), gw), out_shape=...]
where the time goes in v3:
time: 390 us; the launch traced here: 383 us
  Pallas kernels  382 us (98%)
    pallas_call x1, Pallas kernels, front(): pl.pallas_call(functools.partial(front_kernel, n, fused, micro, T, D, FF,...  223 us
    pallas_call x1, Pallas kernels, reduce(): pl.pallas_call(functools.partial(reduce_kernel, n, tok, ls, rs, weights,...  155 us

profile of v3, /device:TPU:0, one launch (start us, length us, event | category | flops | bytes accessed | tf_op | source)
XLA Modules:
  0.0 383.0 jit_solution(10484719251709891444)
XLA Ops:
  0.7 222.8 %shard_map.239 = (bf16[2,256,1024]{2,1,0:T(8,128)(2,1)}, bf16[2,256,1024]{2,1,0:T(8,128)(2,1)}, f32[8,1024]{1,0:T(8,128)}, bf16[2,256,1024]{2,1,0:T(8,128)(2,1)}...) custom-call(bf16[2,256,1024]{2,1,0:T(8,128)(2,1)} %refs_0_.1, ...), custom_call_target="tpu_custom_call" | custom-call | tf_op jit(solution)/shard_map/pallas_call | solution.py:512
  223.5 154.8 %shard_map.240 = (bf16[64,2816]{1,0:T(8,128)(2,1)}, bf16[64,2816]{1,0:T(8,128)(2,1)}, bf16[176,1024]{1,0:T(8,128)(2,1)}, bf16[64,1024]{1,0:T(8,128)(2,1)}, bf16[...) custom-call(bf16[512,2816]{1,0:T(8,128)(2,1)} %bitcast.18, ...), custom_call_target="tpu_custom_call" | custom-call | tf_op jit(solution)/shard_map/pallas_call | solution.py:792
  378.2 4.5 %shard_map.241 = (bf16[1,2,256,1024]{3,2,1,0:T(8,128)(2,1)}, bf16[1,2,256,1024]{3,2,1,0:T(8,128)(2,1)}, bf16[1,64,1024]{2,1,0:T(8,128)(2,1)}, bf16[1,64,1024]{2,...) custom-call(bf16[2,256,1024]{2,1,0:T(8,128)(2,1)} %get-tuple-element, ...), custom_call_target="tpu_custom_call" | custom-call | tf_op jit(solution)/shard_map/pallas_call | solution.py:831

commit v4 on v3

--- a/solution.py
+++ b/solution.py
@@ -188,7 +188,7 @@
     def rows_loop(fn):
         def b(i,_):
             fn(pl.ds(pl.multiple_of(i*RB,RB),RB)); return 0
-        lax.fori_loop(0,T//RB,b,0)
+        lax.fori_loop(0,T//RB,b,0,unroll=T//RB)
     def cols_loop(N,CH,fn):
         def b(i,_):
             fn(pl.ds(pl.multiple_of(i*CH,CH),CH)); return 0
@@ -298,8 +298,9 @@
     first={0:[each(f_norm)],1:[each(lambda m:f_proj(m,q,Wq))],2:[each(lambda m:f_proj(m,k,Wk))],
         3:[each(lambda m:f_proj(m,v,Wv)),lambda:f_attend(0,False)],
         4:[lambda:[f_attend(m,False) for m in range(1,micro)],each(f_out)],
-        6:[each(f_gate)]}
+        6:[lambda:f_gate(0)]}
     for j in range(D//XC): first[7+j]=[down(j)]
+    first[7]=[lambda:[f_gate(m) for m in range(1,micro)]]+first[7]
     units=[(m,kv) for m in range(micro) for kv in range(2)]
     second={i:[functools.partial(recall,*un)] for i,un in enumerate(units)}
     def arrived(i):
@@ -339,7 +340,7 @@
             @pl.when(cond)
             def _():
                 pltpu.make_async_remote_copy(part(i,blk),part(i,blk),s_sb.at[i,kk],r_main.at[i,kk],device_id=dev((z,y,1-c)),device_id_type=MESH).wait_recv()
-        offload=(C==2 and R%2==0)
+        OFF=lambda i: C==2 and R%2==0
         zx=z+1-2*(z%2)
         true=c>=0
         def own(i):
@@ -359,7 +360,7 @@
                     wait_main(ok,i,zbc,y)
                     if sign<0: send(ok&(z<R-1),i,zbc,y,(z+1,y,c),s_zu,r_main)
                     else: send(ok&(z>0),i,zbc,y,(z-1,y,c),s_zd,r_main)
-                    ydo=ok&jnp.logical_not((c==1)&(zbc==zx)) if offload else ok
+                    ydo=ok&jnp.logical_not((c==1)&(zbc==zx)) if OFF(i) else ok
                     send(ydo&(y>0),i,zbc,y,(z,y-1,c),s_yd,r_main)
                     send(ydo&(y<C-1),i,zbc,y,(z,y+1,c),s_yu,r_main)
                     send(ok,i,zbc,y,(z,y,1-c),s_sb,r_sib)
@@ -378,7 +379,7 @@
                             if C>2:
                                 if sign<0: send(ok&(y<C-1),i,zbc,ybc,(z,y+1,c),s_yu,r_main)
                                 else: send(ok&(y>0),i,zbc,ybc,(z,y-1,c),s_yd,r_main)
-                            if offload and d==0:
+                            if OFF(i) and d==0:
                                 send(ok&(c==1),i,zbc,ybc,(zx,y,c),s_ex,r_main)
                             send(ok,i,zbc,ybc,(z,y,1-c),s_sb,r_sib)
         def finish(i):
@@ -519,7 +520,7 @@
 
 
 COLS=1024
-NOFF=99
+NDIRECT=2
 def plan(n, lhs_shapes, rhs_shapes, weights, steps):
     pieces=[]
     for w,(l,r) in enumerate(weights):
@@ -547,7 +548,7 @@
     (ld_sem,sib_s,sib_r,y_s,y_r,x_s,x_r,zu_s,zu_r,zd_s,zd_r,v_s,v_r,o_s)=take(14)
     sec=lax.axis_index("section"); f=lax.axis_index("fsdp")
     c=f%2; zy=f//2; y=zy%C; z=zy//C
-    OFF=lambda i: C==2 and R%2==0 and i<NOFF
+    OFF=lambda i: C==2 and R%2==0
     zx=z+1-2*(z%2)
     def dev(zz,yy,cc): return (sec,(zz*C+yy)*2+cc)
     def rcopy(src,dst,ss,rs,d):
@@ -556,8 +557,7 @@
     nb=[]
     nb.append((c>=0,dev(z,y,1-c)))
     for k in range(1,C): nb.append((c>=0,dev(z,lax.rem(y+k,C),c)))
-    nb.append((z>0,dev(z-1,y,c))); nb.append((z<R-1,dev(z+1,y,c)))
-    for k in range(1,R.bit_length()-1): nb.append((c>=0,(sec,f^(2*C<<k))))
+    for k in range(1,R): nb.append((c>=0,dev(lax.rem(z+k,R),y,c)))
     bar=pltpu.get_barrier_semaphore()
     loads=[]
     def parts(ref,shape):
@@ -690,8 +690,15 @@
                 if offload and kz!=0:
                     pl.when(jnp.logical_not((c==1)&(zt==zx)))(go)
                 else: go()
+    direct=lambda i: i>=NP-NDIRECT
     def z_step(i,s):
         w,rows,c0,nc=pieces[i]
+        if direct(i):
+            if s: return
+            for k in range(1,R):
+                t=lax.rem(z+k,R)
+                send((i,0),None,lambda k=k,t=t: rcopy(keep[i].at[t*C+y],zu[i].at[R-1-k],zu_s.at[i,k-1],zu_r.at[i,R-1-k],(t,y,c)))
+            return
         def line(zs,up):
             rb,rr,ss=(zu,zu_r,zu_s) if up else (zd,zd_r,zd_s)
             first=(zs==0) if up else (zs==R-1)
@@ -714,6 +721,18 @@
     def final(i):
         w,rows,c0,nc=pieces[i]
         blk=z*C+y
+        if direct(i):
+            for k in range(R-1):
+                rcopy(zu[i].at[k],zu[i].at[k],zu_s.at[i,k],zu_r.at[i,k],(z,y,1-c)).wait_recv()
+            def body(j,_):
+                o=pl.ds(pl.multiple_of(j*16,16),16)
+                a=keep[i][blk,o,:].astype(jnp.float32)
+                for k in range(R-1): a=a+zu[i][k,o,:].astype(jnp.float32)
+                fin[i][o,:]=a.astype(jnp.bfloat16)
+                return 0
+            lax.fori_loop(0,rows//16,body,0)
+            pltpu.make_async_copy(fin[i],outs[w].at[:,pl.ds(c0,nc)],o_s.at[i]).start()
+            return
         @pl.when(z>0)
         def _():
             rcopy(zu[i].at[0],zu[i].at[0],zu_s.at[i,0],zu_r.at[i,0],(z,y,1-c)).wait_recv()
@@ -756,7 +775,9 @@
             i=t-LAGY-s
             if 0<=i<NP: z_step(i,s)
         i=t-LAGY-R
-        if 0<=i<NP: final(i)
+        if 0<=i<NP and not direct(i): final(i)
+        i=t-LAGY-1
+        if 0<=i<NP and direct(i): final(i)
         end_sends((t-LAGY-1,'y'))
         for s in range(R): end_sends((t-LAGY-s-2,s))
     for q in sib_waits.values():

time: 390 us -> 384 us (0.985)
  Pallas kernels: 382 us -> 376 us
    pallas_call x1, Pallas kernels: 223 us -> 219 us  [front(): pl.pallas_call(functools.partial(front_kernel, n, fused, micro, T, D, FF,...]
where the time goes in v4:
time: 384 us; the launch traced here: 377 us
  Pallas kernels  376 us (98%)
    pallas_call x1, Pallas kernels, front(): pl.pallas_call(functools.partial(front_kernel, n, fused, micro, T, D, FF,...  219 us
    pallas_call x1, Pallas kernels, reduce(): pl.pallas_call(functools.partial(reduce_kernel, n, tok, ls, rs, weights,...  153 us

profile of v4, /device:TPU:0, one launch (start us, length us, event | category | flops | bytes accessed | tf_op | source)
XLA Modules:
  0.0 377.2 jit_solution(14435013493203697977)
XLA Ops:
  0.7 218.7 %shard_map.239 = (bf16[2,256,1024]{2,1,0:T(8,128)(2,1)}, bf16[2,256,1024]{2,1,0:T(8,128)(2,1)}, f32[8,1024]{1,0:T(8,128)}, bf16[2,256,1024]{2,1,0:T(8,128)(2,1)}...) custom-call(bf16[2,256,1024]{2,1,0:T(8,128)(2,1)} %refs_0_.1, ...), custom_call_target="tpu_custom_call" | custom-call | tf_op jit(solution)/shard_map/pallas_call | solution.py:513
  219.3 152.9 %shard_map.240 = (bf16[64,2816]{1,0:T(8,128)(2,1)}, bf16[64,2816]{1,0:T(8,128)(2,1)}, bf16[176,1024]{1,0:T(8,128)(2,1)}, bf16[64,1024]{1,0:T(8,128)(2,1)}, bf16[...) custom-call(bf16[512,2816]{1,0:T(8,128)(2,1)} %bitcast.18, ...), custom_call_target="tpu_custom_call" | custom-call | tf_op jit(solution)/shard_map/pallas_call | solution.py:813
  372.2 4.5 %shard_map.241 = (bf16[1,2,256,1024]{3,2,1,0:T(8,128)(2,1)}, bf16[1,2,256,1024]{3,2,1,0:T(8,128)(2,1)}, bf16[1,64,1024]{2,1,0:T(8,128)(2,1)}, bf16[1,64,1024]{2,...) custom-call(bf16[2,256,1024]{2,1,0:T(8,128)(2,1)} %get-tuple-element, ...), custom_call_target="tpu_custom_call" | custom-call | tf_op jit(solution)/shard_map/pallas_call | solution.py:852

commit v5 on v4

--- a/solution.py
+++ b/solution.py
@@ -748,6 +748,7 @@
         lax.fori_loop(0,rows//16,body,0)
         pltpu.make_async_copy(fin[i],outs[w].at[:,pl.ds(c0,nc)],o_s.at[i]).start()
     def vec_step(k):
+        if k==0: first_vec.wait()
         if k>0:
             vcopy(k-1).wait()
             vecb[k]=vecb[k-1]+vecr[k-1]
@@ -756,7 +757,7 @@
             cp=pltpu.make_async_copy(vecb.at[LOGN],vec_out,o_s.at[NP]); cp.start()
     def vcopy(k):
         return pltpu.make_async_remote_copy(vecb.at[k],vecr.at[k],v_s.at[k],v_r.at[k],device_id=(sec,f^(1<<k)),device_id_type=MESH)
-    cp=pltpu.make_async_copy(vec,vecb.at[0],o_s.at[NP]); cp.start(); cp.wait()
+    first_vec=pltpu.make_async_copy(vec,vecb.at[0],o_s.at[NP]); first_vec.start()
     pl.semaphore_wait(bar,sum(jnp.where(cond,1,0) for cond,d in nb))
     def end_sends(tag):
         for cond,cp in sends.pop(tag,[]):
@@ -766,9 +767,9 @@
                 def _(cp=cp): cp().wait_send()
     LAGY=3
     for t in range(NP+LAGY+R+1):
+        if 0<=t-2<NP: x_add(t-2)
         if t<NP: compute(t)
         if 0<=t-1<NP: sib_add(t-1)
-        if 0<=t-2<NP: x_add(t-2)
         if t<=LOGN: vec_step(t)
         if 0<=t-LAGY<NP: y_add(t-LAGY)
         for s in range(R):

time: 384 us -> 377 us (0.982)
  Pallas kernels: 376 us -> 369 us
    pallas_call x1, Pallas kernels: 153 us -> 146 us  [reduce(): pl.pallas_call(functools.partial(reduce_kernel, n, tok, ls, rs, weights,...]
where the time goes in v5:
time: 377 us; the launch traced here: 370 us
  Pallas kernels  369 us (98%)
    pallas_call x1, Pallas kernels, front(): pl.pallas_call(functools.partial(front_kernel, n, fused, micro, T, D, FF,...  219 us
    pallas_call x1, Pallas kernels, reduce(): pl.pallas_call(functools.partial(reduce_kernel, n, tok, ls, rs, weights,...  146 us

profile of v5, /device:TPU:0, one launch (start us, length us, event | category | flops | bytes accessed | tf_op | source)
XLA Modules:
  0.0 370.1 jit_solution(1028614723947121043)
XLA Ops:
  0.7 218.6 %shard_map.239 = (bf16[2,256,1024]{2,1,0:T(8,128)(2,1)}, bf16[2,256,1024]{2,1,0:T(8,128)(2,1)}, f32[8,1024]{1,0:T(8,128)}, bf16[2,256,1024]{2,1,0:T(8,128)(2,1)}...) custom-call(bf16[2,256,1024]{2,1,0:T(8,128)(2,1)} %refs_0_.1, ...), custom_call_target="tpu_custom_call" | custom-call | tf_op jit(solution)/shard_map/pallas_call | solution.py:513
  219.3 145.8 %shard_map.240 = (bf16[64,2816]{1,0:T(8,128)(2,1)}, bf16[64,2816]{1,0:T(8,128)(2,1)}, bf16[176,1024]{1,0:T(8,128)(2,1)}, bf16[64,1024]{1,0:T(8,128)(2,1)}, bf16[...) custom-call(bf16[512,2816]{1,0:T(8,128)(2,1)} %bitcast.18, ...), custom_call_target="tpu_custom_call" | custom-call | tf_op jit(solution)/shard_map/pallas_call | solution.py:814
  365.1 4.5 %shard_map.241 = (bf16[1,2,256,1024]{3,2,1,0:T(8,128)(2,1)}, bf16[1,2,256,1024]{3,2,1,0:T(8,128)(2,1)}, bf16[1,64,1024]{2,1,0:T(8,128)(2,1)}, bf16[1,64,1024]{2,...) custom-call(bf16[2,256,1024]{2,1,0:T(8,128)(2,1)} %get-tuple-element, ...), custom_call_target="tpu_custom_call" | custom-call | tf_op jit(solution)/shard_map/pallas_call | solution.py:853
